TPU v7x, 512 devices: a whole 4x8x8 slice. The times are simulated.
512 devices in a mesh: row: 32 (over y, x), col: 16 (over z, core).
Axes of the slice: x: 4, y: 8, z: 8, core: 2. Of those that a mesh axis runs over, the one named last changes fastest.
Arguments:
- features: bfloat16 [65536, 512], P(('col', 'row')), may hold values from -6 to 6
- tile_vals: bfloat16 [32, 64, 256, 256], P('row', 'col')
- tile_rows: int32 [32, 64], P('row', 'col'), may hold values from 0 to 7, as said below
- tile_cols: int32 [32, 64], P('row', 'col'), may hold values from 0 to 15, as said below
- tile_count: int32 [32, 16], P('row', 'col'), may hold values from 1 to 4, as said below
- window: int32 [32, 2], P('row'), may hold values from 0 to 2048, as said below
- w_neigh: bfloat16 [512, 512], replicated, may hold values from -16 to 16
- w_self: bfloat16 [512, 512], replicated, may hold values from -0.25 to 0.25
- layer_bias: float32 [512], replicated, may hold values from -3 to 3
- cotangent: bfloat16 [65536, 512], P(('col', 'row')), may hold values from -6 to 6
Outputs:
- hidden_out: bfloat16 [65536, 512], P(('col', 'row'))
- grad_feat: bfloat16 [65536, 512], P(('col', 'row'))
- grad_neigh: bfloat16 [512, 512], replicated
- grad_self: bfloat16 [512, 512], replicated
- grad_bias: float32 [512], replicated
Inputs may be any that keep to these rules, and one draw needn't show every extreme that they name: `tile_count`: each row block and column block has 2 to 4 live slots; some pair has exactly 4. `tile_rows`: within one row block and column block, slots m and m' name the same tile row only if m - m' is a multiple of 8. `tile_cols`: within one row block and column block, slots m and m' name the same tile column only if m - m' is a multiple of 16. window[r, 0] < window[r, 1]; some row block starts at 0 and some ends at 2048.
All inputs are finite; a program needn't handle non-finite values.
Results may differ from a plain program's by a relative error of at most 0.013.
Values may be sent and summed in bfloat16 or wider, within the bound.
A program may use at most 64 MiB of HBM per device.

v0:
```python
import math

import jax
import jax.numpy as jnp
from jax import lax
from jax.sharding import PartitionSpec as P


def on_device(
    features,
    tile_vals,
    tile_rows,
    tile_cols,
    tile_count,
    window,
    w_neigh,
    w_self,
    layer_bias,
    cotangent,
):
    rows_dev, feat_width = features.shape
    row_devs = lax.axis_size("row")
    col_devs = lax.axis_size("col")
    tile_edge = tile_vals.shape[2]
    slot_count = tile_vals.shape[1]
    col_nodes = row_devs * rows_dev
    row_nodes = col_devs * rows_dev
    col_tiles = col_nodes // tile_edge
    row_tiles = row_nodes // tile_edge
    node_total = row_devs * col_devs * rows_dev
    highest = lax.Precision.HIGHEST
    blocks = tile_vals[0]
    tile_row_ids = tile_rows[0]
    tile_col_ids = tile_cols[0]
    live_slots = (jnp.arange(slot_count, dtype=jnp.int32) < tile_count[0, 0]).astype(jnp.float32)
    row_hot = live_slots[:, None] * (
        tile_row_ids[:, None] == jnp.arange(row_tiles, dtype=jnp.int32)[None, :]
    ).astype(jnp.float32)
    col_hot = live_slots[:, None] * (
        tile_col_ids[:, None] == jnp.arange(col_tiles, dtype=jnp.int32)[None, :]
    ).astype(jnp.float32)
    local_rows = jnp.arange(row_nodes, dtype=jnp.int32)
    inside = ((local_rows >= window[0, 0]) & (local_rows < window[0, 1])).astype(jnp.float32)
    col_panel = lax.all_gather(features, "row", axis=0, tiled=True)
    pieces = col_panel.reshape(col_tiles, tile_edge, feat_width)[tile_col_ids]
    products = jnp.einsum("mij,mjf->mif", blocks, pieces, preferred_element_type=jnp.float32)
    partial_value = jnp.einsum("mt,mif->tif", row_hot, products, precision=highest).reshape(
        row_nodes, feat_width
    )
    partial_value = partial_value * inside[:, None]
    row_totals = jnp.einsum(
        "mij,j->mi",
        blocks,
        jnp.ones((tile_edge,), jnp.bfloat16),
        preferred_element_type=jnp.float32,
    )
    degree_part = (
        jnp.einsum("mt,mi->ti", row_hot, row_totals, precision=highest).reshape(row_nodes) * inside
    )
    got_rows, got_degree = (
        lax.all_to_all(
            partial_value.astype(jnp.bfloat16).reshape(col_devs, rows_dev, feat_width),
            "col",
            split_axis=0,
            concat_axis=0,
            tiled=True,
        ),
        lax.all_to_all(
            degree_part.astype(jnp.bfloat16).reshape(col_devs, rows_dev),
            "col",
            split_axis=0,
            concat_axis=0,
            tiled=True,
        ),
    )
    aggregate = jnp.sum(got_rows.astype(jnp.float32), axis=0)
    degree = jnp.sum(got_degree.astype(jnp.float32), axis=0)
    inverse = 1.0 / (1.0 + degree)
    neigh_rows = (aggregate * inverse[:, None]).astype(jnp.bfloat16)
    preact = jnp.dot(neigh_rows, w_neigh, preferred_element_type=jnp.float32)
    preact = preact + jnp.dot(features, w_self, preferred_element_type=jnp.float32) + layer_bias
    sigmoid_z = jax.nn.sigmoid(preact)
    hidden_out = (preact * sigmoid_z).astype(jnp.bfloat16)
    dpre = cotangent.astype(jnp.float32) * (sigmoid_z * (1.0 + preact * (1.0 - sigmoid_z)))
    dpre_low = dpre.astype(jnp.bfloat16)
    contract = (((0,), (0,)), ((), ()))
    neigh_term = lax.dot_general(neigh_rows, dpre_low, contract, preferred_element_type=jnp.float32)
    self_term = lax.dot_general(features, dpre_low, contract, preferred_element_type=jnp.float32)
    bias_term = jnp.sum(dpre, axis=0)
    sum_neigh, sum_self, sum_bias = lax.psum((neigh_term, self_term, bias_term), ("row", "col"))
    factor = 1.0 / math.sqrt(node_total)
    own_inside = lax.dynamic_slice_in_dim(inside, lax.axis_index("col") * rows_dev, rows_dev, 0)
    back_rows = (
        jnp.dot(dpre_low, w_neigh.T, preferred_element_type=jnp.float32)
        * inverse[:, None]
        * own_inside[:, None]
    )
    back_rows = back_rows.astype(jnp.bfloat16)
    all_back = lax.all_gather(back_rows, "col", axis=0, tiled=True)
    picked = all_back.reshape(row_tiles, tile_edge, feat_width)[tile_row_ids]
    backward = jnp.einsum("mji,mjf->mif", blocks, picked, preferred_element_type=jnp.float32)
    column_part = jnp.einsum("mj,mif->jif", col_hot, backward, precision=highest).reshape(
        col_nodes, feat_width
    )
    got_cols = lax.all_to_all(
        column_part.astype(jnp.bfloat16).reshape(row_devs, rows_dev, feat_width),
        "row",
        split_axis=0,
        concat_axis=0,
        tiled=True,
    )
    neigh_grad = jnp.sum(got_cols.astype(jnp.float32), axis=0)
    self_grad = jnp.dot(dpre_low, w_self.T, preferred_element_type=jnp.float32)
    grad_feat = (self_grad + neigh_grad).astype(jnp.bfloat16)
    grad_neigh = (sum_neigh * factor).astype(jnp.bfloat16)
    grad_self = (sum_self * factor).astype(jnp.bfloat16)
    grad_bias = sum_bias * factor
    return (hidden_out, grad_feat, grad_neigh, grad_self, grad_bias)


def solution(mesh):
    in_specs = (
        P(("col", "row"), None),
        P("row", "col", None, None),
        P("row", "col"),
        P("row", "col"),
        P("row", "col"),
        P("row", None),
        P(),
        P(),
        P(),
        P(("col", "row"), None),
    )
    out_specs = (P(("col", "row"), None), P(("col", "row"), None), P(), P(), P())
    return jax.shard_map(
        on_device, mesh=mesh, in_specs=in_specs, out_specs=out_specs, check_vma=False
    )
```

profile of v0, /device:TPU:1, one launch (start us, length us, event | category | flops | bytes accessed | tf_op | source)
XLA Modules:
  0.0 580.8 jit_solution(1827256199944884260)
XLA Ops:
  7.2 0.0 copy-start
  7.2 0.0 all-gather.3.cloned.1.call-start
  7.2 0.7 all-gather.3.cloned.1.call-update
  8.6 0.0 copy-done
  8.6 0.2 fusion.5
  8.8 0.9 fusion.13
  9.8 1.3 fusion.39
  11.1 1.9 fusion.8
  13.0 11.8 %all-to-all-start.1 = ((bf16[16,1,128]{2,1,0:T(2,128)(2,1)}), bf16[16,1,128]{2,1,0:T(2,128)(2,1)S(1)}, u32[]{:S(2)}, u32[]{:S(2)}) async-start(bf16[16,1,128]{2,1,0:T(2,128)(2,1)} %fusion.8), calls=%async_computation.1 | async-start | bytes 16384 | tf_op jit(solution)/shard_map/all_to_all | solution.py:68
  24.8 0.7 fusion.29
  25.5 1.3 fusion.12
  26.8 74.4 %all-gather.3.cloned.1.call-done = bf16[4096,512]{1,0:T(8,128)(2,1)} async-done(((bf16[128,512]{1,0:T(8,128)(2,1)}), bf16[4096,512]{1,0:T(8,128)(2,1)}) %all-gather.3.cloned.1.call-update) | async-done | bytes 4194320 | tf_op jit(solution)/shard_map/all_gather | solution.py:44
  101.1 3.8 gather_fusion
  104.9 1.7 convolution_bitcast_fusion.1
  106.7 0.0 copy-start.5
  106.7 2.0 copy.26
  108.7 0.0 copy-done.5
  108.7 6.1 %fusion.17 = f32[8,256,512]{2,0,1:T(8,128)S(1)} fusion(f32[4,256,512]{2,0,1:T(4,128)} %copy.26, f32[4]{0:T(128)S(1)} %compare_convert_fusion, s32[4]{0:T(128)S(1)} %bitcast.61), kind=kOutput, calls=%fused_computation.43 | convolution fusion | flops 50331712 | bytes 6291488 | tf_op jit(solution)/shard_map/mt,mif->tif/dot_general | solution.py:47
  114.8 2.4 copy.27
  117.2 1.7 multiply_convert_fusion
  118.9 0.0 all-to-all-done.1
  118.9 10.6 %all-to-all-start = ((bf16[16,128,512]{2,1,0:T(8,128)(2,1)}), bf16[16,128,512]{2,1,0:T(8,128)(2,1)S(1)}, u32[]{:S(2)}, u32[]{:S(2)}) async-start(bf16[16,128,512]{2,1,0:T(8,128)(2,1)} %multiply_convert_fusion), calls=%async_computation | async-start | bytes 4194304 | tf_op jit(solution)/shard_map/all_to_all | solution.py:61
  129.5 0.0 copy-start.1
  129.5 0.2 all-gather.5.cloned.1.call-start
  129.7 1.3 and_convert_fusion
  131.1 47.4 %all-to-all-done = bf16[16,128,512]{2,1,0:T(8,128)(2,1)S(1)} async-done(((bf16[16,128,512]{2,1,0:T(8,128)(2,1)}), bf16[16,128,512]{2,1,0:T(8,128)(2,1)S(1)}, u32[]{:S(2)}, u32[]{:S(2)}) %all-to-all-start) | async-done | bytes 2097184 | tf_op jit(solution)/shard_map/all_to_all | solution.py:61
  178.4 0.0 copy-start.3
  178.4 0.3 convert_reduce_fusion.1
  178.7 0.0 copy-done.1
  178.7 0.0 copy-start.6
  178.7 0.3 fusion.37
  179.0 0.5 copy-done.3
  179.5 2.0 fusion.38
  181.4 1.0 fusion.3
  182.4 0.0 all-gather.5.cloned.1.call-update
  182.4 0.0 copy-done.6
  182.5 38.3 %all-gather.5.cloned.1.call-done = bf16[2048,512]{1,0:T(8,128)(2,1)} async-done(((bf16[128,512]{1,0:T(8,128)(2,1)}), bf16[2048,512]{1,0:T(8,128)(2,1)}) %all-gather.5.cloned.1.call-update) | async-done | bytes 2097168 | tf_op jit(solution)/shard_map/all_gather | solution.py:99
  220.8 3.2 gather_fusion.1
  224.0 1.7 convolution_bitcast_fusion
  225.7 0.0 copy-start.7
  225.7 2.0 copy.30
  227.7 0.0 copy-done.7
  227.8 8.5 %convolution_convert_fusion = bf16[16,256,512]{2,0,1:T(8,128)(2,1)S(1)} fusion(f32[4,256,512]{2,0,1:T(4,128)} %copy.30, f32[4]{0:T(128)S(1)} %compare_convert_fusion, s32[4]{0:T(128)S(1)} %bitcast.62), kind=kOutput, calls=%fused_computation.5 | convolution fusion | flops 102760576 | bytes 6291488 | tf_op jit(solution)/shard_map/mj,mif->jif/dot_general | solution.py:102
  236.2 4.4 copy.31
  240.6 0.0 copy-start.2
  240.6 9.5 %all-to-all-start.2 = ((bf16[32,128,512]{2,1,0:T(8,128)(2,1)}), bf16[32,128,512]{2,1,0:T(8,128)(2,1)}, u32[]{:S(2)}, u32[]{:S(2)}) async-start(bf16[32,128,512]{2,1,0:T(8,128)(2,1)} %bitcast.55), calls=%async_computation.2 | async-start | bytes 8388608 | tf_op jit(solution)/shard_map/all_to_all | solution.py:105
  250.1 0.0 all-reduce.3.cloned.1.call-start
  250.2 0.0 copy-done.2
  250.2 1.3 convolution_bitcast_fusion.2
  251.6 1.4 fusion.36
  252.9 0.0 all-reduce.3.cloned.1.call-update
  252.9 182.9 %psum.23 = f32[512]{0:T(512)S(1)} all-reduce(f32[512]{0:T(512)S(1)} %get-tuple-element.7), channel_id=1, replica_groups=mesh['row'=32,'col'=16] {'row','col'}, use_global_device_ids=true, to_apply=%region_6.0 | all-reduce | flops 512 | bytes 4096 | tf_op jit(solution)/shard_map/psum | solution.py:90
  435.9 0.6 broadcast_multiply_fusion
  436.4 131.2 %all-reduce.3.cloned.1.call-done = (f32[512,512]{1,0:T(8,128)}, f32[512,512]{1,0:T(8,128)}) async-done(((f32[512,512]{1,0:T(8,128)}, f32[512,512]{1,0:T(8,128)}), (f32[512,512]{1,0:T(8,128)}, f32[512,512]{1,0:T(8,128)})) %all-reduce.3.cloned.1.call-update) | async-done | bytes 2097168 | tf_op jit(solution)/shard_map/psum | solution.py:90
  567.7 2.8 multiply_convert_fusion.1
  570.4 0.0 copy-start.4
  570.4 0.0 all-to-all-done.2
  570.4 2.9 convert_reduce_fusion
  573.3 0.0 copy-done.4
  573.3 1.0 fusion.2
  (7 shorter events, 0.1 us)
Async XLA Ops:
  7.2 1.4 copy-start
  7.2 94.0 %all-gather.3.cloned.1.call-start = ((), (), s32[]{:S(2)}) async-start(), calls=%async_computation.3 | async-start | bytes 4325376 | tf_op jit(solution)/shard_map/all_gather | solution.py:44
  13.0 105.9 %all-to-all-start.1 = ((bf16[16,1,128]{2,1,0:T(2,128)(2,1)}), bf16[16,1,128]{2,1,0:T(2,128)(2,1)S(1)}, u32[]{:S(2)}, u32[]{:S(2)}) async-start(bf16[16,1,128]{2,1,0:T(2,128)(2,1)} %fusion.8), calls=%async_computation.1 | async-start | bytes 16384 | tf_op jit(solution)/shard_map/all_to_all | solution.py:68
  106.7 2.0 copy-start.5
  118.9 59.5 %all-to-all-start = ((bf16[16,128,512]{2,1,0:T(8,128)(2,1)}), bf16[16,128,512]{2,1,0:T(8,128)(2,1)S(1)}, u32[]{:S(2)}, u32[]{:S(2)}) async-start(bf16[16,128,512]{2,1,0:T(8,128)(2,1)} %multiply_convert_fusion), calls=%async_computation | async-start | bytes 4194304 | tf_op jit(solution)/shard_map/all_to_all | solution.py:61
  129.5 49.2 %copy-start.1 = (bf16[512,512]{1,0:T(8,128)(2,1)S(1)}, bf16[512,512]{1,0:T(8,128)(2,1)}, u32[]{:S(2)}) copy-start(bf16[512,512]{1,0:T(8,128)(2,1)} %param.16) | copy-start | bytes 1572868
  129.5 91.3 %all-gather.5.cloned.1.call-start = ((), (), s32[]{:S(2)}) async-start(), calls=%async_computation.4 | async-start | bytes 2228224 | tf_op jit(solution)/shard_map/all_gather | solution.py:99
  178.4 1.0 copy-start.3
  178.7 3.7 copy-start.6
  225.7 2.0 copy-start.7
  240.6 9.6 %copy-start.2 = (bf16[128,512]{1,0:T(8,128)(2,1)S(1)}, bf16[128,512]{1,0:T(8,128)(2,1)}, u32[]{:S(2)}) copy-start(bf16[128,512]{1,0:T(8,128)(2,1)} %param.10) | copy-start | bytes 393220
  240.6 329.8 %all-to-all-start.2 = ((bf16[32,128,512]{2,1,0:T(8,128)(2,1)}), bf16[32,128,512]{2,1,0:T(8,128)(2,1)}, u32[]{:S(2)}, u32[]{:S(2)}) async-start(bf16[32,128,512]{2,1,0:T(8,128)(2,1)} %bitcast.55), calls=%async_computation.2 | async-start | bytes 8388608 | tf_op jit(solution)/shard_map/all_to_all | solution.py:105
  250.1 317.5 %all-reduce.3.cloned.1.call-start = ((), (), s32[]{:S(2)}) async-start(), calls=%async_computation.5 | async-start | bytes 4194304 | tf_op jit(solution)/shard_map/psum | solution.py:90
  570.4 2.9 copy-start.4
Sparse Core Ops, SparseCore 0:
  11.2 89.9 all-gather.2
  182.5 38.1 all-gather.4
  256.1 311.5 all-reduce.2
where the time goes:
time: 581 us
  waiting for transfers between devices  292 us (50%)
  blocking collectives  183 us (31%)
  starting transfers between devices  32.2 us (6%)
  matrix products  26.1 us (4%)
  local copies, waits for them, and re-layouts  19.6 us (3%)
  between operations  14.6 us (3%)
  other arithmetic  13.4 us (2%)
    psum x1, blocking collectives, on_device(): lax.psum((neigh_term, self_term, bias_term), ('row', 'col'))  183 us
    psum x1, waiting for transfers between devices, on_device(): lax.psum((neigh_term, self_term, bias_term), ('row', 'col'))  131 us
    all_gather x1, waiting for transfers between devices, on_device(): col_panel = lax.all_gather(features, 'row', axis=0, tiled=True)  74.4 us
    all_to_all x1, waiting for transfers between devices, on_device(): lax.all_to_all(partial_value.astype(jnp.bfloat16).reshape(col_devs, rows_...  47.4 us
    all_gather x1, waiting for transfers between devices, on_device(): all_back = lax.all_gather(back_rows, 'col', axis=0, tiled=True)  38.3 us
    all_to_all x1, starting transfers between devices, on_device(): lax.all_to_all(degree_part.astype(jnp.bfloat16).reshape(col_devs, rows_de...  11.8 us
  transfers between devices with their start and end apart: 6, of which 4 were waited for; matrix products, arithmetic and copies ran while one was open for 5% of the time, Pallas kernels for 0%

commit v1 on v0

v1 whole, which is shorter than its diff:
```python
import functools
import heapq
import math

import jax
import jax.numpy as jnp
from jax import lax
from jax.experimental import pallas as pl
from jax.experimental.pallas import tpu as pltpu
from jax.sharding import PartitionSpec as P

MESH = pl.DeviceIdType.MESH
BF = jnp.bfloat16
F32 = jnp.float32

NX = 4
ROUNDS = 2
ROWS = 128
HALF = ROWS // 2
LANES = 128
SEMS = 256
HOP = 1.5
UNIT = 0.65


def nn(a, b):
    return jnp.dot(a, b, preferred_element_type=F32)


def nt(a, b):
    return lax.dot_general(a, b, (((1,), (1,)), ((), ())), preferred_element_type=F32)


class Plan:
    def __init__(self):
        self.heap, self.count, self.now = [], 0, 0.0

    def spawn(self, chain, when):
        heapq.heappush(self.heap, (when, self.count, chain))
        self.count += 1

    def run(self):
        while self.heap:
            when, _, chain = heapq.heappop(self.heap)
            self.now = max(self.now, when)
            try:
                later = next(chain)
            except StopIteration:
                continue
            self.spawn(chain, later)


class Join:
    def __init__(self, count, then):
        self.count, self.then, self.when = count, then, 0.0

    def done(self, when):
        self.count -= 1
        self.when = max(self.when, when)
        if self.count == 0:
            self.then(self.when)


class Links:
    def __init__(self, send, recv):
        self.send, self.recv, self.used, self.sent = send, recv, 0, []

    def start(self, src, dst, device):
        at = self.used
        self.used += 1
        copy = pltpu.make_async_remote_copy(
            src_ref=src,
            dst_ref=dst,
            send_sem=self.send.at[at],
            recv_sem=self.recv.at[at],
            device_id=device,
            device_id_type=MESH,
        )
        copy.start()
        self.sent.append(copy)
        return copy

    def finish(self):
        for copy in self.sent:
            copy.wait_send()


class Direct:
    def __init__(self, links, size, me, device, src, dst):
        self.links, self.size, self.me = links, size, me
        self.device, self.src, self.dst = device, src, dst
        self.base = links.used
        links.used += size - 1
        links.sent.append(self)

    def copy(self, step):
        other = lax.rem(self.me + step, self.size)
        return pltpu.make_async_remote_copy(
            src_ref=self.src(other),
            dst_ref=self.dst(self.me),
            send_sem=self.links.send.at[self.base + step - 1],
            recv_sem=self.links.recv.at[self.base + step - 1],
            device_id=self.device(other),
            device_id_type=MESH,
        )

    def start(self):
        @pl.loop(1, self.size)
        def _(step):
            self.copy(step).start()

    def wait_recv(self):
        @pl.loop(1, self.size)
        def _(step):
            self.copy(step).wait_recv()

    def wait_send(self):
        @pl.loop(1, self.size)
        def _(step):
            self.copy(step).wait_send()


def gather_chain(links, way, size, me, block, device, begin, hop, done):
    steps = size // 2
    clock, copy = begin, None
    for step in range(1, steps + 1):
        if copy is not None:
            clock += hop
            yield clock
            copy.wait_recv()
        owner = lax.rem(me - way * (step - 1) + size, size)
        part = None if step < steps else (0 if way > 0 else 1)
        ref = block(owner, part)
        copy = links.start(ref, ref, device(lax.rem(me + way + size, size)))
    clock += hop
    yield clock
    copy.wait_recv()
    done(clock)


def scatter_chain(links, way, size, me, block, slot, add, device, begin, hop, done):
    steps = size // 2
    clock, copy = begin, None
    half = 0 if way > 0 else 1
    for step in range(1, steps + 1):
        owner = lax.rem(me + way * (steps - step + 1) + size, size)
        part = half if step == 1 else None
        if copy is not None:
            clock += hop
            yield clock
            copy.wait_recv()
            was = half if step == 2 else None
            add(block(owner, was), slot(step - 1, was))
        copy = links.start(
            block(owner, part), slot(step, part), device(lax.rem(me + way + size, size))
        )
    clock += hop
    yield clock
    copy.wait_recv()
    done(clock)


def add_into(to, frm):
    to[...] = to[...] + frm[...]


def layer(
    sizes,
    feat,
    tiles,
    tile_rows,
    tile_cols,
    tile_count,
    window,
    w_neigh,
    w_self,
    bias,
    cot,
    hidden_out,
    gfeat_out,
    gneigh_out,
    gself_out,
    gbias_out,
    *scratch,
):
    names = list(scratch)

    def take():
        return names.pop(0)

    NY, NZ, SLOTS, EDGE, WIDTH = sizes
    NC = 2 * NZ
    XH = NX // 2
    CW = 2 * LANES
    panel = [take() for _ in range(ROUNDS)]
    part = [take() for _ in range(ROUNDS)]
    pair = [take() for _ in range(ROUNDS)]
    zslot = [take() for _ in range(ROUNDS)]
    back = [take() for _ in range(ROUNDS)]
    colp = [take() for _ in range(ROUNDS)]
    ry0 = [take() for _ in range(ROUNDS)]
    rx0 = [take() for _ in range(ROUNDS)]
    rx1 = [take() for _ in range(ROUNDS)]
    ry1 = [take() for _ in range(ROUNDS)]
    tile = take()
    turned = take()
    featv, cotv, wnv, wsv = take(), take(), take(), take()
    deg_own, deg_all = take(), take()
    own_in, inv = take(), take()
    pre = take()
    selfg = take()
    lhs, lhs_in = take(), take()
    dlow, dlow_in = take(), take()
    dbias, dbias_in = take(), take()
    ez, ez_in = take(), take()
    bz_in = take()
    ey, ey_in = take(), take()
    ex, ex_in = take(), take()
    ag = take()
    grads = take()
    hid, gft = take(), take()
    send, recv, local = take(), take(), take()
    assert not names

    r, c = lax.axis_index("row"), lax.axis_index("col")
    y, x = r // NX, lax.rem(r, NX)
    z, k = c // 2, lax.rem(c, 2)
    mate = 1 - k

    def at_x(i):
        return {"row": y * NX + i}

    def at_y(i):
        return {"row": i * NX + x}

    def at_z(i):
        return {"col": i * 2 + k}

    def at_c(i):
        return {"col": i}

    partner = {"col": z * 2 + mate}

    loads = []

    def load(src, dst):
        copy = pltpu.make_async_copy(src, dst, local.at[len(loads)])
        copy.start()
        loads.append(copy)
        return copy

    own = []
    for q in range(ROUNDS):
        for h in range(2):
            cols = pl.ds((2 * q + h) * LANES, LANES)
            own.append(load(feat.at[:, cols], panel[q].at[h, y, x]))
    tile_load = load(tiles.at[0], tile.at[pl.ds(0, SLOTS)])
    feat_load = load(feat, featv)
    ws_load = load(w_self, wsv)
    wn_load = load(w_neigh, wnv)
    cot_load = load(cot, cotv)

    barrier = pltpu.get_barrier_semaphore()

    @pl.loop(1, NX)
    def _(i):
        pl.semaphore_signal(barrier, inc=1, device_id=at_x(lax.rem(x + i, NX)), device_id_type=MESH)

    @pl.loop(1, NY)
    def _(i):
        pl.semaphore_signal(barrier, inc=1, device_id=at_y(lax.rem(y + i, NY)), device_id_type=MESH)

    @pl.loop(1, NC)
    def _(i):
        pl.semaphore_signal(barrier, inc=1, device_id=at_c(lax.rem(c + i, NC)), device_id_type=MESH)

    pl.semaphore_wait(barrier, NX + NY + NC - 3)

    links, plan = Links(send, recv), Plan()
    for copy in own:
        copy.wait()

    lo, hi = window[0, 0], window[0, 1]
    count = tile_count[0, 0]
    slot_row = [tile_rows[0, m] for m in range(SLOTS)]
    slot_col = [tile_cols[0, m] for m in range(SLOTS)]

    def slot_of(ids, want):
        found = jnp.int32(SLOTS)
        for m in range(SLOTS):
            found = jnp.where((ids[m] == want) & (m < count), m, found)
        return found

    def value_at(ids, m):
        found = ids[0]
        for i in range(1, SLOTS):
            found = jnp.where(m == i, ids[i], found)
        return found

    def rows2(ref, *lead):
        return lambda owner, p: (
            ref.at[(*lead, owner)]
            if p is None
            else ref.at[(*lead, owner, pl.ds(HALF * p, HALF))]
        )

    def gather0(q, begin):
        def rows_then(when):
            end = Join(2, lambda t: ready_a[q].done(t))
            for way in (1, -1):

                def block(o, p):
                    if p is None:
                        return panel[q].at[0, o]
                    return panel[q].at[0, o, pl.ds(XH * p, XH)]

                plan.spawn(
                    gather_chain(links, way, NY, y, block, at_y, when, HOP + NX * UNIT, end.done),
                    when,
                )

        mid = Join(2, rows_then)
        for way in (1, -1):
            plan.spawn(
                gather_chain(links, way, NX, x, rows2(panel[q], 0, y), at_x, begin, HOP + UNIT, mid.done),
                begin,
            )

    def gather1(q, begin):
        def cols_then(when):
            end = Join(2, lambda t: ready_a[q].done(t))
            for way in (1, -1):

                def block(o, p):
                    if p is None:
                        return panel[q].at[1, :, o]
                    return panel[q].at[1, pl.ds(NY // 2 * p, NY // 2), o]

                plan.spawn(
                    gather_chain(links, way, NX, x, block, at_x, when, HOP + NY * UNIT, end.done),
                    when,
                )

        def block(o, p):
            if p is None:
                return panel[q].at[1, o, x]
            return panel[q].at[1, o, x, pl.ds(HALF * p, HALF)]

        mid = Join(2, cols_then)
        for way in (1, -1):
            plan.spawn(
                gather_chain(links, way, NY, y, block, at_y, begin, HOP + UNIT, mid.done),
                begin,
            )

    def prepare(when):
        yield when
        tile_load.wait()
        tile[SLOTS] = jnp.zeros((EDGE, EDGE), BF)

        @pl.loop(0, SLOTS + 1)
        def _(m):
            turned[m] = tile[m].T

        lane = lax.broadcasted_iota(jnp.int32, (8, EDGE), 1)

        @pl.loop(0, NZ)
        def _(t):
            total = nn(jnp.ones((8, EDGE), BF), turned[slot_of(slot_row, t)])
            at = lane + t * EDGE
            total = jnp.where((at >= lo) & (at < hi), total, 0.0)
            deg_own[2 * t] = total[:, :ROWS]
            deg_own[2 * t + 1] = total[:, ROWS:]

        deg_all[c] = deg_own[c]
        degree.start()
        yield when + 0.5
        feat_load.wait()
        ws_load.wait()
        pre[...] = nn(featv[...], wsv[...]) + bias[...]
        lhs[1] = featv[...]
        at = lax.broadcasted_iota(jnp.int32, (ROWS, LANES), 0) + c * ROWS
        own_in[...] = jnp.where((at >= lo) & (at < hi), 1.0, 0.0)
        yield when + 12.0
        degree.wait_recv()
        total = deg_all[0]
        for i in range(1, NC):
            total = total + deg_all[i]
        inverse = 1.0 / (1.0 + total)
        inv[...] = jnp.tile(inverse, (ROWS // 8, 1)).T
        wn_load.wait()
        cot_load.wait()

    degree = Direct(links, NC, c, at_c, lambda o: deg_own.at[o], lambda i: deg_all.at[i])

    def forward(q, when):
        yield when

        @pl.loop(0, NZ)
        def _(t):
            m = slot_of(slot_row, t)
            j = value_at(slot_col, m)
            yy, xx = j // XH, lax.rem(j, XH) * 2
            left = panel[q][0, yy, pl.ds(xx, 2)].reshape(EDGE, LANES)
            right = panel[q][1, yy, pl.ds(xx, 2)].reshape(EDGE, LANES)
            out = nn(tile[m], jnp.concatenate([left, right], axis=1))
            at = lax.broadcasted_iota(jnp.int32, (EDGE, CW), 0) + t * EDGE
            out = jnp.where((at >= lo) & (at < hi), out, 0.0).astype(BF)
            part[q][0, t] = out[:ROWS]
            part[q][1, t] = out[ROWS:]

        swap = links.start(part[q].at[mate], pair[q], partner)
        when = max(when, plan.now) + 4.0
        yield when
        swap.wait_recv()

        @pl.loop(0, NZ)
        def _(t):
            pair[q][t] = pair[q][t] + part[q][k, t]

        end = Join(2, lambda t: ready_b.done(t))
        for way in (1, -1):
            w = 0 if way > 0 else 1

            def slot(step, p, w=w):
                if p is None:
                    return zslot[q].at[w, step - 1]
                return zslot[q].at[w, step - 1, pl.ds(HALF * p, HALF)]

            plan.spawn(
                scatter_chain(
                    links, way, NZ, z, rows2(pair[q]), slot, add_into, at_z, when, HOP + 2 * UNIT, end.done
                ),
                when,
            )

    def middle(when):
        yield when
        last = NZ // 2 - 1
        wide = jnp.concatenate([inv[...], inv[...]], axis=1)
        for q in range(ROUNDS):
            total = pair[q][z].astype(F32) + zslot[q][0, last].astype(F32) + zslot[q][1, last].astype(F32)
            low = (total * wide).astype(BF)
            lhs[0, :, q * CW : (q + 1) * CW] = low
            pre[...] += nn(low, wnv[q * CW : (q + 1) * CW, :])
        value = pre[...]
        s = jax.nn.sigmoid(value)
        hid[...] = (value * s).astype(BF)
        hidden_store.start()
        dpre = cotv[...].astype(F32) * (s * (1.0 + value * (1.0 - s)))
        low = dpre.astype(BF)
        dlow[...] = low
        scale = wide * jnp.concatenate([own_in[...], own_in[...]], axis=1)
        for q in range(ROUNDS):
            out = nt(low, wnv[q * CW : (q + 1) * CW, :]) * scale
            back[q][z, k] = out.astype(BF)
        when = max(when, plan.now) + 2.0
        for q in range(ROUNDS):
            spread(q, when + 0.1 * q)
        total = dpre[0:8]
        for i in range(1, ROWS // 8):
            total = total + dpre[8 * i : 8 * i + 8]
        dbias[...] = total
        plan.spawn(gradients(when), when + 0.5)
        yield when + 1.0
        selfg[...] = nt(dlow[...], wsv[...])

    hidden_store = pltpu.make_async_copy(hid, hidden_out, local.at[9])

    def spread(q, when):
        def chain(way, begin, done):
            steps = NZ // 2
            clock, copy = begin, None
            for step in range(1, steps + 2):
                owner = lax.rem(z - way * (step - 1) + NZ, NZ)
                was = None if step <= steps else (0 if way > 0 else 1)
                now = None if step < steps else (0 if way > 0 else 1)
                if copy is not None:
                    clock += HOP + 2 * UNIT
                    yield clock
                    copy.wait_recv()
                if step <= steps:
                    ref = block(owner, now)
                    copy = links.start(ref, ref, at_z(lax.rem(z + way + NZ, NZ)))
                if step > 1 or way > 0:
                    ref = block(owner, was)
                    mates.append(links.start(ref, ref, partner))
            done(clock)

        def block(o, p):
            if p is None:
                return back[q].at[o, k]
            return back[q].at[o, k, pl.ds(HALF * p, HALF)]

        mates = []
        end = Join(2, lambda t: plan.spawn(backward(q, t + HOP, mates), t + HOP))
        for way in (1, -1):
            plan.spawn(chain(way, when, end.done), when)

    def backward(q, when, mates):
        yield when
        for copy in mates:
            copy.wait_recv()

        @pl.loop(0, NY * XH)
        def _(j):
            m = slot_of(slot_col, j)
            t = value_at(slot_row, m)
            out = nn(turned[m], back[q][t].reshape(EDGE, CW)).astype(BF)
            yy, xx = j // XH, lax.rem(j, XH) * 2
            for h in range(2):
                for i in range(2):
                    colp[q][h, yy, xx + i] = out[i * ROWS : (i + 1) * ROWS, h * LANES : (h + 1) * LANES]

        when = max(when, plan.now) + 2.0
        scatter0(q, when)
        scatter1(q, when)

    def scatter0(q, begin):
        last_y, last_x = NY // 2 - 1, NX // 2 - 1

        def finish(when):
            write(q, 0, rx0[q][0, last_x], rx0[q][1, last_x])
            ready_d.done(when)

        def then(when):
            for w in range(2):
                add_into(colp[q].at[0, y], ry0[q].at[w, last_y])
            end = Join(2, finish)
            for way in (1, -1):
                w = 0 if way > 0 else 1

                def slot(step, p, w=w):
                    if p is None:
                        return rx0[q].at[w, step - 1]
                    return rx0[q].at[w, step - 1, pl.ds(HALF * p, HALF)]

                plan.spawn(
                    scatter_chain(
                        links, way, NX, x, rows2(colp[q], 0, y), slot, add_into, at_x, when, HOP + UNIT, end.done
                    ),
                    when,
                )

        mid = Join(2, then)
        for way in (1, -1):
            w = 0 if way > 0 else 1

            def block(o, p):
                if p is None:
                    return colp[q].at[0, o]
                return colp[q].at[0, o, pl.ds(XH * p, XH)]

            def slot(step, p, w=w):
                if p is None:
                    return ry0[q].at[w, step - 1]
                return ry0[q].at[w, step - 1, pl.ds(XH * p, XH)]

            plan.spawn(
                scatter_chain(links, way, NY, y, block, slot, add_into, at_y, begin, HOP + NX * UNIT, mid.done),
                begin,
            )

    def scatter1(q, begin):
        last_y, last_x = NY // 2 - 1, NX // 2 - 1

        def finish(when):
            write(q, 1, ry1[q][0, last_y], ry1[q][1, last_y])
            ready_d.done(when)

        def then(when):
            for w in range(2):
                add_into(colp[q].at[1, :, x], rx1[q].at[w, last_x])
            end = Join(2, finish)
            for way in (1, -1):
                w = 0 if way > 0 else 1

                def block(o, p):
                    if p is None:
                        return colp[q].at[1, o, x]
                    return colp[q].at[1, o, x, pl.ds(HALF * p, HALF)]

                def slot(step, p, w=w):
                    if p is None:
                        return ry1[q].at[w, step - 1]
                    return ry1[q].at[w, step - 1, pl.ds(HALF * p, HALF)]

                plan.spawn(
                    scatter_chain(links, way, NY, y, block, slot, add_into, at_y, when, HOP + UNIT, end.done),
                    when,
                )

        mid = Join(2, then)
        for way in (1, -1):
            w = 0 if way > 0 else 1
            deep = NY // 2

            def block(o, p):
                if p is None:
                    return colp[q].at[1, :, o]
                return colp[q].at[1, pl.ds(deep * p, deep), o]

            def slot(step, p, w=w):
                if p is None:
                    return rx1[q].at[w, step - 1]
                return rx1[q].at[w, step - 1, pl.ds(deep * p, deep)]

            plan.spawn(
                scatter_chain(links, way, NX, x, block, slot, add_into, at_x, begin, HOP + NY * UNIT, mid.done),
                begin,
            )

    def write(q, h, one, two):
        cols = slice((2 * q + h) * LANES, (2 * q + h + 1) * LANES)
        total = colp[q][h, y, x].astype(F32) + one.astype(F32) + two.astype(F32)
        gft[:, cols] = (total + selfg[:, cols]).astype(BF)

    def gradients(when):
        yield when
        swaps = [
            links.start(lhs.at[mate], lhs_in, partner),
            links.start(dlow, dlow_in, partner),
            links.start(dbias, dbias_in, partner),
        ]
        yield when + 4.0
        for copy in swaps:
            copy.wait_recv()
        bz_in[z] = dbias[...] + dbias_in[...]
        both = jnp.concatenate([dlow[...], dlow_in[...]], axis=0)
        deep = WIDTH // NZ

        wide = WIDTH // 4
        for i in range(4):
            cut = slice(i * wide, (i + 1) * wide)
            left = jnp.concatenate([lhs[k, :, cut], lhs_in[:, cut]], axis=0)
            out = nn(left.T, both)
            for j in range(wide // deep):
                ez[i * (wide // deep) + j] = out[j * deep : (j + 1) * deep].astype(BF)
        ez_in[z] = ez[z]
        sum_z.start()
        bias_z.start()
        yield when + 16.0
        sum_z.wait_recv()
        bias_z.wait_recv()
        total = ez_in[0].astype(F32)
        for i in range(1, NZ):
            total = total + ez_in[i].astype(F32)
        low = bz_in[0]
        for i in range(1, NZ):
            low = low + bz_in[i]
        for i in range(NY):
            ey[i, 0:8] = total[8 * i : 8 * i + 8]
            ey[i, 8:16] = low
        ey_in[y] = ey[y]
        sum_y.start()
        yield when + 21.0
        sum_y.wait_recv()
        total = ey_in[0]
        for i in range(1, NY):
            total = total + ey_in[i]
        ex[...] = total
        ex_in[x] = total
        sum_x.start()
        yield when + 26.0
        sum_x.wait_recv()
        total = ex_in[0]
        for i in range(1, NX):
            total = total + ex_in[i]
        total = total * factor
        gbias_out[...] = jnp.sum(total[8:16], axis=0, keepdims=True)
        ag[y] = total[0:8]
        all_y.start()
        yield when + 31.0
        all_y.wait_recv()
        grads[k, z] = jnp.concatenate([ag[i] for i in range(NY)], axis=0).astype(BF)
        all_z.start()
        yield when + 42.0
        all_z.wait_recv()
        last = links.start(grads.at[k], grads.at[k], partner)
        yield when + 45.0
        last.wait_recv()
        ready_e.done(when + 45.0)

    factor = 1.0 / math.sqrt(ROWS * NY * NX * NC)
    sum_z = Direct(links, NZ, z, at_z, lambda o: ez.at[o], lambda i: ez_in.at[i])
    bias_z = Direct(links, NZ, z, at_z, lambda o: bz_in.at[z], lambda i: bz_in.at[i])
    sum_y = Direct(links, NY, y, at_y, lambda o: ey.at[o], lambda i: ey_in.at[i])
    sum_x = Direct(links, NX, x, at_x, lambda o: ex, lambda i: ex_in.at[i])
    all_y = Direct(links, NY, y, at_y, lambda o: ag.at[y], lambda i: ag.at[i])
    all_z = Direct(links, NZ, z, at_z, lambda o: grads.at[k, z], lambda i: grads.at[k, i])

    ready_a = [Join(2, lambda t, q=q: plan.spawn(forward(q, t), t)) for q in range(ROUNDS)]
    ready_b = Join(ROUNDS, lambda t: plan.spawn(middle(t), t))
    ready_d = Join(2 * ROUNDS, lambda t: None)
    ready_e = Join(1, lambda t: None)
    for q in range(ROUNDS):
        gather0(q, 0.05 * q)
        gather1(q, 0.05 * q)
    plan.spawn(prepare(0.5), 0.5)
    plan.run()

    stores = [
        pltpu.make_async_copy(gft, gfeat_out, local.at[10]),
        pltpu.make_async_copy(grads.at[0], gneigh_out, local.at[11]),
        pltpu.make_async_copy(grads.at[1], gself_out, local.at[12]),
    ]
    for copy in stores:
        copy.start()
    links.finish()
    hidden_store.wait()
    for copy in stores:
        copy.wait()


def on_device(
    features, tile_vals, tile_rows, tile_cols, tile_count, window, w_neigh, w_self, layer_bias, cotangent
):
    rows, width = features.shape
    slots, edge = tile_vals.shape[1:3]
    ny = lax.axis_size("row") // NX
    nz = lax.axis_size("col") // 2
    nc = 2 * nz

    def vmem(*shape, dtype=BF):
        return pltpu.VMEM(shape, dtype)

    cw = 2 * LANES
    each = [
        (2, ny, NX, ROWS, LANES),
        (2, nz, ROWS, cw),
        (nz, ROWS, cw),
        (2, nz // 2, ROWS, cw),
        (nz, 2, ROWS, cw),
        (2, ny, NX, ROWS, LANES),
        (2, ny // 2, NX, ROWS, LANES),
        (2, NX // 2, ROWS, LANES),
        (2, NX // 2, ny, ROWS, LANES),
        (2, ny // 2, ROWS, LANES),
    ]
    deep = width // nz
    scratch = [vmem(*shape) for shape in each for _ in range(ROUNDS)]
    scratch += [vmem(slots + 1, edge, edge)] * 2
    scratch += [vmem(rows, width), vmem(rows, width), vmem(width, width), vmem(width, width)]
    scratch += [vmem(nc, 8, ROWS, dtype=F32)] * 2
    scratch += [vmem(ROWS, LANES, dtype=F32)] * 2
    scratch += [vmem(rows, width, dtype=F32)] * 2
    scratch += [vmem(2, rows, width), vmem(rows, width)]
    scratch += [vmem(rows, width)] * 2
    scratch += [vmem(8, width, dtype=F32)] * 2
    scratch += [vmem(nz, deep, width)] * 2
    scratch += [vmem(nz, 8, width, dtype=F32)]
    scratch += [vmem(ny, 16, width, dtype=F32)] * 2
    scratch += [vmem(16, width, dtype=F32), vmem(NX, 16, width, dtype=F32)]
    scratch += [vmem(ny, 8, width, dtype=F32)]
    scratch += [vmem(2, nz, deep, width)]
    scratch += [vmem(rows, width)] * 2
    scratch += [pltpu.SemaphoreType.DMA((SEMS,))] * 2 + [pltpu.SemaphoreType.DMA((16,))]
    anywhere = pl.BlockSpec(memory_space=pl.ANY)
    small = pl.BlockSpec(memory_space=pltpu.SMEM)
    fast = pl.BlockSpec(memory_space=pltpu.VMEM)
    sizes = (ny, nz, slots, edge, width)
    hidden, gfeat, gneigh, gself, gbias = pl.pallas_call(
        functools.partial(layer, sizes),
        out_shape=(
            jax.ShapeDtypeStruct((rows, width), BF),
            jax.ShapeDtypeStruct((rows, width), BF),
            jax.ShapeDtypeStruct((nz, deep, width), BF),
            jax.ShapeDtypeStruct((nz, deep, width), BF),
            jax.ShapeDtypeStruct((1, width), F32),
        ),
        in_specs=[anywhere, anywhere, small, small, small, small, anywhere, anywhere, fast, anywhere],
        out_specs=(anywhere, anywhere, anywhere, anywhere, fast),
        scratch_shapes=scratch,
        compiler_params=pltpu.CompilerParams(
            collective_id=0, has_side_effects=True, vmem_limit_bytes=48 * 1024 * 1024
        ),
    )(
        features,
        tile_vals,
        tile_rows,
        tile_cols,
        tile_count,
        window,
        w_neigh,
        w_self,
        layer_bias.reshape(1, width),
        cotangent,
    )
    return hidden, gfeat, gneigh.reshape(width, width), gself.reshape(width, width), gbias.reshape(width)


def solution(mesh):
    in_specs = (
        P(("col", "row"), None),
        P("row", "col", None, None),
        P("row", "col"),
        P("row", "col"),
        P("row", "col"),
        P("row", None),
        P(),
        P(),
        P(),
        P(("col", "row"), None),
    )
    out_specs = (P(("col", "row"), None), P(("col", "row"), None), P(), P(), P())
    return jax.shard_map(
        on_device, mesh=mesh, in_specs=in_specs, out_specs=out_specs, check_vma=False
    )
```

time: 581 us -> 168 us (0.29)
  waiting for transfers between devices: 292 us -> 0 us
  blocking collectives: 183 us -> 0 us
  Pallas kernels: 0 us -> 158 us
  starting transfers between devices: 32.2 us -> 0 us
  matrix products: 26.1 us -> 0 us
  other arithmetic: 13.4 us -> 0 us
  between operations: 14.6 us -> 1.35 us
  local copies, waits for them, and re-layouts: 19.6 us -> 9.06 us
    psum x1 -> x0, blocking collectives: 183 us -> none  [on_device(): lax.psum((neigh_term, self_term, bias_term), ('row', 'col'))]
    pallas_call x0 -> x1, Pallas kernels: none -> 158 us  [on_device(): pl.pallas_call(functools.partial(layer, sizes), out_shape=(jax.ShapeDtype...]
    psum x1 -> x0, waiting for transfers between devices: 131 us -> none  [on_device(): lax.psum((neigh_term, self_term, bias_term), ('row', 'col'))]
    all_gather x2 -> x0, waiting for transfers between devices: 113 us -> none  [the longest x1 74.4 us: on_device(): col_panel = lax.all_gather(features, 'row', axis=0, tiled=True)]
    all_to_all x3 -> x0, waiting for transfers between devices: 47.4 us -> none  [the longest x1 47.4 us: on_device(): lax.all_to_all(partial_value.astype(jnp.bfloat16).reshape(col_devs, rows_...]
    all_to_all x3 -> x0, starting transfers between devices: 31.9 us -> none  [the longest x1 11.8 us: on_device(): lax.all_to_all(degree_part.astype(jnp.bfloat16).reshape(col_devs, rows_de...]
    dot_general x12 -> x0, matrix products: 26.1 us -> none  [the longest x1 8.49 us: on_device(): jnp.einsum('mj,mif->jif', col_hot, backward, precision=highest)]
    convert_element_type x6 -> x0, other arithmetic: 8.95 us -> none  [the longest x1 2.77 us: on_device(): grad_self = (sum_self * factor).astype(jnp.bfloat16)]
  transfers between devices with their start and end apart: 6 -> 0, of which waited for: 4 -> 0; matrix products, arithmetic and copies ran while one was open for 5% -> 0% of each run, Pallas kernels for 0% -> 0%
where the time goes in v1:
time: 168 us
  Pallas kernels  158 us (94%)
  local copies, waits for them, and re-layouts  9.06 us (5%)
    pallas_call x1, Pallas kernels, on_device(): pl.pallas_call(functools.partial(layer, sizes), out_shape=(jax.ShapeDtype...  158 us
    unnamed x23, local copies, waits for them, and re-layouts  9.06 us

profile of v1, /device:TPU:1, one launch (start us, length us, event | category | flops | bytes accessed | tf_op | source)
XLA Modules:
  0.0 167.9 jit_solution(12945053006157633586)
XLA Ops:
  0.6 0.0 copy-start.5
  1.3 0.0 copy-start.6
  1.3 0.0 copy-start.7
  1.3 0.0 copy-start.8
  1.3 0.0 copy-done.5
  1.3 0.6 copy-done.6
  2.0 0.0 copy-done.7
  2.0 0.0 copy-done.8
  2.0 0.0 copy-start
  2.0 1.0 copy-done
  3.0 0.0 copy-start.1
  3.0 1.0 copy-done.1
  4.1 0.0 copy-start.2
  4.1 1.0 copy-done.2
  5.1 0.0 copy-start.3
  5.1 0.9 copy-done.3
  6.0 0.0 copy-start.4
  6.0 0.9 copy-done.4
  6.9 157.5 %shard_map.137 = (bf16[128,512]{1,0:T(8,128)(2,1)S(1)}, bf16[128,512]{1,0:T(8,128)(2,1)S(1)}, bf16[8,64,512]{2,1,0:T(8,128)(2,1)S(1)}, bf16[8,64,512]{2,1,0:T(8,128)(2,1)S(1)}, f32[1,512]{1,0:T(1,128)S(1)}) custom-call(bf16[128,512]{1,0:T(8,128)(2,1)S(1)} %copy-done.3, bf16[1,4,256,256]{3,2,1,0:T(8,128)(2,1)S(1)} %copy-done, s32[1,4]{1,0:T(1,128)S(1)} %copy-done.6, ...), custom_call_target="tpu_custom_call" | custom-call | tf_op jit(solution)/shard_map/pallas_call | solution.py:762
  164.5 0.7 copy.21
  165.1 0.7 copy.22
  165.8 0.8 copy.23
  166.6 0.8 copy.24
  167.4 0.6 copy.25
Async XLA Ops:
  0.6 0.7 copy-start.5
  1.3 0.7 copy-start.6
  1.3 0.7 copy-start.7
  1.3 0.7 copy-start.8
  2.0 1.0 copy-start
  3.0 1.0 copy-start.1
  4.1 1.0 copy-start.2
  5.1 0.9 copy-start.3
  6.0 0.9 copy-start.4

commit v2 on v0

v2 whole, which is shorter than its diff:
```python
import functools
import heapq
import math

import jax
import jax.numpy as jnp
from jax import lax
from jax.experimental import pallas as pl
from jax.experimental.pallas import tpu as pltpu
from jax.sharding import PartitionSpec as P

MESH = pl.DeviceIdType.MESH
BF = jnp.bfloat16
F32 = jnp.float32

NX = 4
FWD = ((256, False), (256, False),)
BWD = ((256, False), (256, False),)
STAGGER = 0
ROWS = 128
HALF = ROWS // 2
LANES = 128
SEMS = 400
VMEM_LIMIT = 63 * 1024 * 1024
LINK_RATE, HOP = 88e3, 1.6
CORE_RATE, CORE_HOP = 350e3, 0.9
ISSUE = 0.07
PLANE = 3.5


def nn(a, b):
    return jnp.dot(a, b, preferred_element_type=F32)


def nt(a, b):
    return lax.dot_general(a, b, (((1,), (1,)), ((), ())), preferred_element_type=F32)


class Plan:
    def __init__(self):
        self.heap, self.count, self.now, self.idle = [], 0, 0.0, []

    def spawn(self, chain, when):
        heapq.heappush(self.heap, (when, self.count, chain))
        self.count += 1

    def later(self, cost, work):
        self.idle.append((cost, work))

    def flush(self):
        while self.idle:
            cost, work = self.idle.pop(0)
            work()
            self.now += cost

    def run(self):
        while self.heap or self.idle:
            if self.idle and (not self.heap or self.heap[0][0] > self.now + self.idle[0][0]):
                cost, work = self.idle.pop(0)
                work()
                self.now += cost
                continue
            when, _, chain = heapq.heappop(self.heap)
            self.now = max(self.now, when)
            try:
                self.spawn(chain, next(chain))
            except StopIteration:
                pass


class Join:
    def __init__(self, count, then):
        self.count, self.then = count, then

    def done(self):
        self.count -= 1
        if self.count == 0:
            self.then()


class Links:
    def __init__(self, plan, send, recv):
        self.plan, self.send, self.recv, self.used, self.sent = plan, send, recv, 0, []
        self.free = {}

    def start(self, src, dst, device, link, hops=1):
        at = self.used
        self.used += 1
        copy = pltpu.make_async_remote_copy(
            src_ref=src,
            dst_ref=dst,
            send_sem=self.send.at[at],
            recv_sem=self.recv.at[at],
            device_id=device,
            device_id_type=MESH,
        )
        copy.start()
        self.sent.append(copy)
        size = math.prod(src.shape) * src.dtype.itemsize
        rate, hop = (CORE_RATE, CORE_HOP) if link == "core" else (LINK_RATE / 2, HOP)
        self.plan.now += ISSUE
        ready = max(self.plan.now, self.free.get(link, 0.0)) + hops * size / rate
        self.free[link] = ready
        return copy, ready + hop + 0.3 * (hops - 1)

    def finish(self):
        for copy in self.sent:
            copy.wait_send()


class Direct:
    def __init__(self, links, size, me, device, src, dst):
        self.links, self.size, self.me = links, size, me
        self.device, self.src, self.dst = device, src, dst
        self.base = links.used
        links.used += size - 1
        links.sent.append(self)

    def copy(self, step):
        other = lax.rem(self.me + step, self.size)
        return pltpu.make_async_remote_copy(
            src_ref=self.src(other),
            dst_ref=self.dst(self.me),
            send_sem=self.links.send.at[self.base + step - 1],
            recv_sem=self.links.recv.at[self.base + step - 1],
            device_id=self.device(other),
            device_id_type=MESH,
        )

    def start(self):
        @pl.loop(1, self.size)
        def _(step):
            self.copy(step).start()

        self.links.plan.now += ISSUE * self.size

    def wait_recv(self):
        @pl.loop(1, self.size)
        def _(step):
            self.copy(step).wait_recv()

    def wait_send(self):
        @pl.loop(1, self.size)
        def _(step):
            self.copy(step).wait_send()


def gather_chain(links, axis, way, size, me, block, device, done, pass_on=None):
    steps, held = size // 2, None
    half = 0 if way > 0 else 1
    for step in range(1, steps + 2):
        owner = lax.rem(me - way * (step - 1) + size, size)
        if held is not None:
            yield held[1]
            held[0].wait_recv()
        if step <= steps:
            ref = block(owner, None if step < steps else half)
            held = links.start(ref, ref, device(lax.rem(me + way + size, size)), (axis, way))
        if pass_on is not None and (step > 1 or way > 0):
            pass_on(block(owner, None if step <= steps else half))
    done()


def scatter_chain(links, axis, way, size, me, block, slot, device, done):
    steps, held = size // 2, None
    half = 0 if way > 0 else 1
    for step in range(1, steps + 1):
        owner = lax.rem(me + way * (steps - step + 1) + size, size)
        part = half if step == 1 else None
        if held is not None:
            yield held[1]
            held[0].wait_recv()
            was = half if step == 2 else None
            add_into(block(owner, was), slot(step - 1, was))
            links.plan.now += 0.2
        held = links.start(
            block(owner, part), slot(step, part), device(lax.rem(me + way + size, size)), (axis, way)
        )
    yield held[1]
    held[0].wait_recv()
    done()


def add_into(to, frm):
    to[...] = to[...] + frm[...]


def layer(
    sizes,
    feat,
    tiles,
    rows_in,
    cols_in,
    count_in,
    window_in,
    w_neigh,
    w_self,
    bias_in,
    cot,
    hidden_out,
    gfeat_out,
    grads_out,
    gbias_out,
    *scratch,
):
    names = list(scratch)

    def take():
        return names.pop(0)

    NY, NZ, SLOTS, EDGE, WIDTH = sizes
    NC, NR = 2 * NZ, NX * NY
    XH = NX // 2
    DEEP = WIDTH // NZ
    fwd, bwd = range(len(FWD)), range(len(BWD))
    fwd_at = [sum(w for w, _ in FWD[:q]) for q in fwd]
    bwd_at = [sum(w for w, _ in BWD[:q]) for q in bwd]
    panel = [take() for _ in fwd]
    part = [take() for _ in fwd]
    pair = [take() for _ in fwd]
    zslot = [take() for _ in fwd]
    prod = [take() for _ in fwd]
    back = [take() for _ in bwd]
    back_prod = [take() for _ in bwd]
    colp = [take() for _ in bwd]
    ry0 = [take() for _ in bwd]
    rx0 = [take() for _ in bwd]
    rx1 = [take() for _ in bwd]
    ry1 = [take() for _ in bwd]
    tile = take()
    turned = take()
    featv, cotv, wnv, wsv = take(), take(), take(), take()
    bias = take()
    deg_own, deg_all = take(), take()
    own_in, inv = take(), take()
    pre = take()
    selfg = take()
    lhs, lhs_in = take(), take()
    dlow, dlow_in = take(), take()
    dbias, dbias_in = take(), take()
    ez, ez_in = take(), take()
    bz_in = take()
    ex, ex_in = take(), take()
    ey, ey_in = take(), take()
    ag = take()
    grads = take()
    hid, gft, gb = take(), take(), take()
    tile_rows, tile_cols, tile_count, window = take(), take(), take(), take()
    send, recv, local = take(), take(), take()
    assert not names

    r, c = lax.axis_index("row"), lax.axis_index("col")
    y, x = r // NX, lax.rem(r, NX)
    z, k = c // 2, lax.rem(c, 2)
    mate = 1 - k

    def at_x(i):
        return {"row": y * NX + i}

    def at_y(i):
        return {"row": i * NX + x}

    def at_z(i):
        return {"col": i * 2 + k}

    def at_c(i):
        return {"col": i}

    partner = {"col": z * 2 + mate}

    loads = []

    def load(src, dst):
        copy = pltpu.make_async_copy(src, dst, local.at[len(loads)])
        copy.start()
        loads.append(copy)
        return copy

    barrier = pltpu.get_barrier_semaphore()

    @pl.loop(1, NX)
    def _(i):
        pl.semaphore_signal(barrier, inc=1, device_id=at_x(lax.rem(x + i, NX)), device_id_type=MESH)

    @pl.loop(1, NY)
    def _(i):
        pl.semaphore_signal(barrier, inc=1, device_id=at_y(lax.rem(y + i, NY)), device_id_type=MESH)

    @pl.loop(1, NC)
    def _(i):
        pl.semaphore_signal(barrier, inc=1, device_id=at_c(lax.rem(c + i, NC)), device_id_type=MESH)

    own = []
    for q in fwd:
        own.append(load(feat.at[:, pl.ds(fwd_at[q], FWD[q][0])], panel[q].at[y, x]))
    scalars = [
        load(rows_in, tile_rows),
        load(cols_in, tile_cols),
        load(count_in, tile_count),
        load(window_in, window),
    ]
    tile_load = load(tiles.at[0], tile.at[pl.ds(0, SLOTS)])
    feat_load = load(feat, featv)
    ws_load = load(w_self, wsv)
    bias_load = load(bias_in, bias)
    wn_load = load(w_neigh, wnv)
    cot_load = load(cot, cotv)
    for copy in own + scalars:
        copy.wait()

    pl.semaphore_wait(barrier, NX + NY + NC - 3)

    plan = Plan()
    links = Links(plan, send, recv)
    lo, hi = window[0, 0], window[0, 1]
    count = tile_count[0, 0]
    slot_row = [tile_rows[0, m] for m in range(SLOTS)]
    slot_col = [tile_cols[0, m] for m in range(SLOTS)]

    def slot_of(ids, want):
        found = jnp.int32(SLOTS)
        for m in range(SLOTS):
            found = jnp.where((ids[m] == want) & (m < count), m, found)
        return found

    def cut(ref, half):
        def view(*at):
            *lead, p = at
            if p is None:
                return ref.at[tuple(lead)]
            return ref.at[(*lead, pl.ds(half * p, half))]

        return view

    def far(d, size):
        d = d if d <= size // 2 else d - size
        return d, 1 if d > 0 else -1

    def straight(axis, size, me, device, src, dst):
        copies = []
        for d in sorted(range(1, size), key=lambda d: -abs(far(d, size)[0])):
            other = lax.rem(me + d, size)
            steps, way = far(d, size)
            copies.append(links.start(src(other), dst(me), device(other), (axis, way), abs(steps)))
        return copies

    top, low_rows = pl.ds(0, HALF), HALF // 2

    def gather0(q):
        def view(o, p):
            if p is None:
                return panel[q].at[o, :, top]
            return panel[q].at[o, pl.ds(XH * p, XH), top]

        mine = panel[q].at[y, x, top]
        copies = straight("x", NX, x, at_x, lambda o: mine, lambda i: mine)
        yield max(when for _, when in copies)
        for copy, _ in copies:
            copy.wait_recv()
        for way in (1, -1):
            plan.spawn(gather_chain(links, "y", way, NY, y, view, at_y, ready_a[q].done), plan.now)

    def gather1(q):
        deep = NY // 2

        def view(o, p):
            if p is None:
                return panel[q].at[:, o, pl.ds(HALF, HALF)]
            return panel[q].at[pl.ds(deep * p, deep), o, pl.ds(HALF, HALF)]

        def cols_then():
            for way in (1, -1):
                plan.spawn(gather_chain(links, "x", way, NX, x, view, at_x, ready_a[q].done), plan.now)

        def inner(o, p):
            if p is None:
                return panel[q].at[o, x, pl.ds(HALF, HALF)]
            return panel[q].at[o, x, pl.ds(HALF + low_rows * p, low_rows)]

        mid = Join(2, cols_then)
        for way in (1, -1):
            plan.spawn(gather_chain(links, "y", way, NY, y, inner, at_y, mid.done), plan.now)

    def gather(q):
        yield STAGGER * q
        plan.spawn(gather0(q), plan.now)
        gather1(q)

    def take_tiles():
        tile_load.wait()
        tile[SLOTS] = jnp.zeros((EDGE, EDGE), BF)
        turned[SLOTS] = jnp.zeros((EDGE, EDGE), BF)
        for q in fwd:
            prod[q][SLOTS] = jnp.zeros((EDGE, FWD[q][0]), BF)
        for q in bwd:
            back_prod[q][SLOTS] = jnp.zeros((EDGE, BWD[q][0]), BF)

    def turn(m):
        turned[m] = tile[m].T

    def degrees():
        lane = lax.broadcasted_iota(jnp.int32, (8, EDGE), 1)

        @pl.loop(0, NZ)
        def _(t):
            total = nn(jnp.ones((8, EDGE), BF), turned[slot_of(slot_row, t)])
            at = lane + t * EDGE
            total = jnp.where((at >= lo) & (at < hi), total, 0.0)
            deg_own[2 * t] = total[:, :ROWS]
            deg_own[2 * t + 1] = total[:, ROWS:]

        deg_all[c] = deg_own[c]
        degree.start()

    def self_term():
        feat_load.wait()
        ws_load.wait()
        bias_load.wait()
        pre[...] = nn(featv[...], wsv[...]) + bias[...]
        lhs[1] = featv[...]
        at = lax.broadcasted_iota(jnp.int32, (ROWS, LANES), 0) + c * ROWS
        own_in[...] = jnp.where((at >= lo) & (at < hi), 1.0, 0.0)

    def invert():
        yield 18.0
        degree.wait_recv()
        total = deg_all[0]
        for i in range(1, NC):
            total = total + deg_all[i]
        inverse = 1.0 / (1.0 + total)
        inv[...] = jnp.tile(inverse, (ROWS // 8, 1)).T
        wn_load.wait()
        cot_load.wait()
        plan.now += 0.5

    degree = Direct(links, NC, c, at_c, lambda o: deg_own.at[o], lambda i: deg_all.at[i])

    def forward(q):
        wide, direct = FWD[q]
        yield plan.now
        plan.flush()

        @pl.loop(0, SLOTS)
        def _(m):
            j = tile_cols[0, m]
            yy, xx = j // XH, lax.rem(j, XH) * 2
            prod[q][m] = nn(tile[m], panel[q][yy, pl.ds(xx, 2)].reshape(EDGE, wide)).astype(BF)

        end = Join(2, ready_b.done)
        swaps = {}
        order = [NZ // 2]
        for d in range(NZ // 2 - 1, 0, -1):
            order += [d, -d]
        order.append(0)
        for d in order:
            t = lax.rem(z + d + NZ, NZ)
            out = prod[q][slot_of(slot_row, t)]
            at = lax.broadcasted_iota(jnp.int32, (EDGE, wide), 0) + t * EDGE
            out = jnp.where((at >= lo) & (at < hi), out, jnp.zeros_like(out))
            part[q][0, t] = out[:ROWS]
            part[q][1, t] = out[ROWS:]
            swaps[d] = links.start(part[q].at[mate, t], pair[q].at[t], partner, "core")
            plan.now += 0.1

        def meet(d):
            copy, when = swaps.pop(d)
            yield when
            copy.wait_recv()
            t = lax.rem(z + d + NZ, NZ)
            pair[q][t] = pair[q][t] + part[q][k, t]

        def chain(way):
            steps, held = NZ // 2, None
            half = 0 if way > 0 else 1
            slot, block = cut(zslot[q], HALF), cut(pair[q], HALF)
            for step in range(1, steps + 1):
                d = way * (steps - step + 1)
                owner = lax.rem(z + d + NZ, NZ)
                if d in swaps:
                    yield from meet(d)
                now = half if step == 1 else None
                if held is not None:
                    yield held[1]
                    held[0].wait_recv()
                    was = half if step == 2 else None
                    add_into(block(owner, was), slot(half * steps + step - 2, was))
                    plan.now += 0.2
                held = links.start(
                    block(owner, now),
                    slot(half * steps + step - 1, now),
                    at_z(lax.rem(z + way + NZ, NZ)),
                    ("z", way),
                )
            yield held[1]
            held[0].wait_recv()
            if 0 in swaps:
                yield from meet(0)
            end.done()

        def direct_chain():
            copies = []
            for d in order:
                yield from meet(d)
                if d != 0:
                    way = 1 if d > 0 else -1
                    t = lax.rem(z + d + NZ, NZ)
                    copies.append(links.start(pair[q].at[t], zslot[q].at[z], at_z(t), ("z", way), abs(d)))
            yield max(when for _, when in copies)
            for copy, _ in copies:
                copy.wait_recv()
            ready_b.done()

        def ring():
            yield from meet(NZ // 2)
            for way in (1, -1):
                plan.spawn(chain(way), plan.now)

        if direct:
            plan.spawn(direct_chain(), plan.now)
        else:
            plan.spawn(ring(), plan.now)

    def middle():
        yield plan.now
        half = NZ // 2
        for q in fwd:
            wide, direct = FWD[q]
            total = pair[q][z].astype(F32)
            if direct:
                for d in range(1, NZ):
                    total = total + zslot[q][lax.rem(z + d, NZ)].astype(F32)
            else:
                total = total + zslot[q][half - 1].astype(F32) + zslot[q][2 * half - 1].astype(F32)
            low = (total * jnp.tile(inv[...], (1, wide // LANES))).astype(BF)
            cols = slice(fwd_at[q], fwd_at[q] + wide)
            lhs[0, :, cols] = low
            pre[...] += nn(low, wnv[cols, :])
        value = pre[...]
        s = jax.nn.sigmoid(value)
        dpre = cotv[...].astype(F32) * (s * (1.0 + value * (1.0 - s)))
        low = dpre.astype(BF)
        dlow[...] = low
        scale = inv[...] * own_in[...]
        plan.now += 1.5
        for q in bwd:
            wide = BWD[q][0]
            out = nt(low, wnv[bwd_at[q] : bwd_at[q] + wide, :]) * jnp.tile(scale, (1, wide // LANES))
            back[q][z, k] = out.astype(BF)
            plan.now += 0.4
            spread(q)
        total = jnp.sum(dpre, axis=0, keepdims=True)
        lanes = [total[:, i * LANES : (i + 1) * LANES] for i in range(WIDTH // LANES)]
        dbias[...] = jnp.concatenate(lanes + [jnp.zeros((8 - len(lanes), LANES), F32)], axis=0)
        hid[...] = (value * s).astype(BF)
        hidden_store.start()
        plan.now += 0.4
        plan.spawn(gradients(), plan.now)

        def self_back():
            selfg[...] = nt(dlow[...], wsv[...])

        plan.later(0.7, self_back)

    hidden_store = pltpu.make_async_copy(hid, hidden_out, local.at[15])

    def spread(q):
        mates = []
        view = cut(back[q], HALF)

        def pass_on(ref):
            mates.append(links.start(ref, ref, partner, "core"))

        def then():
            plan.spawn(backward(q, mates), max(when for _, when in mates))

        def direct_chain():
            mine = back[q].at[z, k]
            pass_on(mine)
            copies = []
            for d in sorted(range(1, NZ), key=lambda d: -abs(far(d, NZ)[0])):
                other = lax.rem(z + d, NZ)
                steps, way = far(d, NZ)
                copies.append((d, *links.start(mine, mine, at_z(other), ("z", way), abs(steps))))
            for d, copy, when in sorted(copies, key=lambda item: item[2]):
                yield when
                copy.wait_recv()
                pass_on(back[q].at[lax.rem(z - d + NZ, NZ), k])
            then()

        if BWD[q][1]:
            plan.spawn(direct_chain(), plan.now)
            return
        end = Join(2, then)
        for way in (1, -1):
            chain = gather_chain(
                links, "z", way, NZ, z, lambda o, p: view(o, k, p), at_z, end.done, pass_on
            )
            plan.spawn(chain, plan.now)

    def backward(q, mates):
        yield plan.now
        plan.flush()
        for copy, _ in mates:
            copy.wait_recv()
        wide = BWD[q][0]

        @pl.loop(0, SLOTS)
        def _(m):
            t = tile_rows[0, m]
            back_prod[q][m] = nn(turned[m], back[q][t].reshape(EDGE, wide)).astype(BF)

        @pl.loop(0, NY * XH)
        def _(j):
            out = back_prod[q][slot_of(slot_col, j)]
            yy, xx = j // XH, lax.rem(j, XH) * 2
            for i in range(2):
                colp[q][yy, xx + i] = out[i * ROWS : (i + 1) * ROWS]

        plan.now += 2.0
        scatter0(q)
        scatter1(q)

    def scatter0(q):
        last_y = NY // 2 - 1

        def tail():
            copies = straight("x", NX, x, at_x, lambda o: colp[q].at[y, o, top], lambda i: rx0[q].at[i])
            yield max(when for _, when in copies)
            for copy, _ in copies:
                copy.wait_recv()
            write(q, 0, [rx0[q][lax.rem(x + d, NX)] for d in range(1, NX)])

        def then():
            for w in range(2):
                add_into(colp[q].at[y, :, top], ry0[q].at[w, last_y])
            plan.spawn(tail(), plan.now)

        def block(o, p):
            if p is None:
                return colp[q].at[o, :, top]
            return colp[q].at[o, pl.ds(XH * p, XH), top]

        mid = Join(2, then)
        slot = cut(ry0[q], XH)
        for w, way in enumerate((1, -1)):
            chain = scatter_chain(
                links, "y", way, NY, y, block, lambda step, p, w=w: slot(w, step - 1, p), at_y, mid.done
            )
            plan.spawn(chain, plan.now)

    def scatter1(q):
        last_y, last_x = NY // 2 - 1, NX // 2 - 1
        deep = NY // 2
        bottom = pl.ds(HALF, HALF)

        def finish():
            write(q, 1, [ry1[q][last_y], ry1[q][NY - 1]])

        def inner(o, p):
            if p is None:
                return colp[q].at[o, x, bottom]
            return colp[q].at[o, x, pl.ds(HALF + low_rows * p, low_rows)]

        def then():
            for w in range(2):
                add_into(colp[q].at[:, x, bottom], rx1[q].at[w, last_x])
            end = Join(2, finish)
            slot = cut(ry1[q], low_rows)
            for w, way in enumerate((1, -1)):
                chain = scatter_chain(
                    links,
                    "y",
                    way,
                    NY,
                    y,
                    inner,
                    lambda step, p, w=w: slot(w * (NY // 2) + step - 1, p),
                    at_y,
                    end.done,
                )
                plan.spawn(chain, plan.now)

        def block(o, p):
            if p is None:
                return colp[q].at[:, o, bottom]
            return colp[q].at[pl.ds(deep * p, deep), o, bottom]

        mid = Join(2, then)
        slot = cut(rx1[q], deep)
        for w, way in enumerate((1, -1)):
            chain = scatter_chain(
                links, "x", way, NX, x, block, lambda step, p, w=w: slot(w, step - 1, p), at_x, mid.done
            )
            plan.spawn(chain, plan.now)

    def write(q, h, terms):
        rows, cols = slice(HALF * h, HALF * (h + 1)), slice(bwd_at[q], bwd_at[q] + BWD[q][0])
        total = colp[q][y, x, rows].astype(F32)
        for term in terms:
            total = total + term.astype(F32)
        gft[rows, cols] = (total + selfg[rows, cols]).astype(BF)

    def gradients():
        swaps = [
            links.start(lhs.at[mate], lhs_in, partner, "core"),
            links.start(dlow, dlow_in, partner, "core"),
            links.start(dbias, dbias_in, partner, "core"),
        ]
        yield swaps[-1][1]
        for copy, _ in swaps:
            copy.wait_recv()
        bz_in[z] = dbias[...] + dbias_in[...]
        bias_z.start()
        yield plan.now
        wide = WIDTH // 4
        for i in range(4):
            at = slice(i * wide, (i + 1) * wide)
            left = jnp.concatenate([lhs[k, :, at], lhs_in[:, at]], axis=0)
            both = jnp.concatenate([dlow[...], dlow_in[...]], axis=0)
            out = nn(left.T, both)
            for j in range(wide // DEEP):
                ez[i * (wide // DEEP) + j] = out[j * DEEP : (j + 1) * DEEP].astype(BF)
            plan.now += 0.4
            yield plan.now
        end = Join(2, lambda: plan.spawn(plane_sum(), plan.now))
        block, slot = cut(ez, DEEP // 2), cut(ez_in, DEEP // 2)
        for w, way in enumerate((1, -1)):
            plan.spawn(
                scatter_chain(
                    links,
                    "z",
                    way,
                    NZ,
                    z,
                    block,
                    lambda step, p, w=w: slot(w, step - 1, p),
                    at_z,
                    end.done,
                ),
                plan.now,
            )

    def plane_sum():
        yield plan.now
        bias_z.wait_recv()
        last = NZ // 2 - 1
        total = ez[z].astype(F32) + ez_in[0, last].astype(F32) + ez_in[1, last].astype(F32)
        low = bz_in[0]
        for i in range(1, NZ):
            low = low + bz_in[i]
        for j in range(NX):
            ex[j, 0:DEEP] = total[:, j * LANES : (j + 1) * LANES]
            ex[j, DEEP : DEEP + 8] = low
        ex_in[x] = ex[x]
        sum_x.start()
        yield plan.now + PLANE
        sum_x.wait_recv()
        total = ex_in[0]
        for i in range(1, NX):
            total = total + ex_in[i]
        for i in range(NY):
            ey[i, 0:8] = total[8 * i : 8 * i + 8]
            ey[i, 8:16] = total[DEEP : DEEP + 8]
        ey_in[y] = ey[y]
        sum_y.start()
        yield plan.now + PLANE
        sum_y.wait_recv()
        total = ey_in[0]
        for i in range(1, NY):
            total = total + ey_in[i]
        total = total * factor
        ag[y] = total[0:8]
        all_y.start()
        for j in range(WIDTH // LANES):
            gb[:, j * LANES : (j + 1) * LANES] = total[8 + j : 9 + j]
        yield plan.now + PLANE
        all_y.wait_recv()
        low = jnp.concatenate([ag[i] for i in range(NY)], axis=0).astype(BF)
        grads[k, z, :, lanes_of(x)] = low
        all_x.start()
        yield plan.now + PLANE
        all_x.wait_recv()
        mates = []
        end = Join(2, lambda: plan.spawn(collect(mates), max(when for _, when in mates)))
        view = cut(grads, DEEP // 2)
        for way in (1, -1):
            chain = gather_chain(
                links,
                "z",
                way,
                NZ,
                z,
                lambda o, p: view(k, o, p),
                at_z,
                end.done,
                lambda ref: mates.append(links.start(ref, ref, partner, "core")),
            )
            plan.spawn(chain, plan.now)

    def collect(mates):
        yield plan.now
        for copy, _ in mates:
            copy.wait_recv()

    factor = 1.0 / math.sqrt(ROWS * NR * NC)
    bias_z = Direct(links, NZ, z, at_z, lambda o: bz_in.at[z], lambda i: bz_in.at[i])
    sum_x = Direct(links, NX, x, at_x, lambda o: ex.at[o], lambda i: ex_in.at[i])
    sum_y = Direct(links, NY, y, at_y, lambda o: ey.at[o], lambda i: ey_in.at[i])
    all_y = Direct(links, NY, y, at_y, lambda o: ag.at[y], lambda i: ag.at[i])

    def lanes_of(i):
        return pl.ds(pl.multiple_of(i * LANES, LANES), LANES)

    all_x = Direct(
        links,
        NX,
        x,
        at_x,
        lambda o: grads.at[k, z, :, lanes_of(x)],
        lambda i: grads.at[k, z, :, lanes_of(i)],
    )

    ready_a = [Join(4, lambda q=q: plan.spawn(forward(q), plan.now)) for q in fwd]
    ready_b = Join(len(FWD), lambda: plan.spawn(middle(), plan.now))
    for q in fwd:
        plan.spawn(gather(q), STAGGER * q)
    plan.later(0.4, take_tiles)
    for m in range(SLOTS):
        plan.later(0.3, functools.partial(turn, m))
    plan.later(1.5, degrees)
    plan.later(1.0, self_term)
    plan.spawn(invert(), 10.0)
    plan.run()
    assert links.used <= SEMS

    stores = [
        pltpu.make_async_copy(gft, gfeat_out, local.at[16]),
        pltpu.make_async_copy(grads, grads_out, local.at[17]),
        pltpu.make_async_copy(gb, gbias_out, local.at[18]),
    ]
    for copy in stores:
        copy.start()
    links.finish()
    hidden_store.wait()
    for copy in stores:
        copy.wait()


def write_out(hidden, gfeat, grads, gbias, hidden_out, gfeat_out, gneigh_out, gself_out, gbias_out, *scratch):
    *held, sems = scratch
    sources = [grads.at[0], grads.at[1], hidden, gfeat, gbias]
    targets = [gneigh_out, gself_out, hidden_out, gfeat_out, gbias_out]
    count = len(held)
    takes = [pltpu.make_async_copy(a, b, sems.at[i]) for i, (a, b) in enumerate(zip(sources, held))]
    gives = [pltpu.make_async_copy(a, b, sems.at[count + i]) for i, (a, b) in enumerate(zip(held, targets))]
    for copy in takes:
        copy.start()
    for take, give in zip(takes, gives):
        take.wait()
        give.start()
    for copy in gives:
        copy.wait()


def on_device(
    features, tile_vals, tile_rows, tile_cols, tile_count, window, w_neigh, w_self, layer_bias, cotangent
):
    rows, width = features.shape
    slots, edge = tile_vals.shape[1:3]
    ny = lax.axis_size("row") // NX
    nz = lax.axis_size("col") // 2
    nc = 2 * nz

    def vmem(*shape, dtype=BF):
        return pltpu.VMEM(shape, dtype)

    fwd, bwd = [w for w, _ in FWD], [w for w, _ in BWD]
    each = [
        (fwd, (ny, NX, ROWS)),
        (fwd, (2, nz, ROWS)),
        (fwd, (nz, ROWS)),
        (fwd, (nz, ROWS)),
        (fwd, (slots + 1, edge)),
        (bwd, (nz, 2, ROWS)),
        (bwd, (slots + 1, edge)),
        (bwd, (ny, NX, ROWS)),
        (bwd, (2, ny // 2, NX, HALF)),
        (bwd, (NX, HALF)),
        (bwd, (2, NX // 2, ny, HALF)),
        (bwd, (ny, HALF)),
    ]
    deep = width // nz
    scratch = [vmem(*shape, w) for widths, shape in each for w in widths]
    scratch += [vmem(slots + 1, edge, edge)] * 2
    scratch += [vmem(rows, width), vmem(rows, width), vmem(width, width), vmem(width, width)]
    scratch += [vmem(1, width, dtype=F32)]
    scratch += [vmem(nc, 8, ROWS, dtype=F32)] * 2
    scratch += [vmem(ROWS, LANES, dtype=F32)] * 2
    scratch += [vmem(rows, width, dtype=F32)] * 2
    scratch += [vmem(2, rows, width), vmem(rows, width)]
    scratch += [vmem(rows, width)] * 2
    scratch += [vmem(8, LANES, dtype=F32)] * 2
    scratch += [vmem(nz, deep, width), vmem(2, nz // 2, deep, width)]
    scratch += [vmem(nz, 8, LANES, dtype=F32)]
    scratch += [vmem(NX, deep + 8, LANES, dtype=F32)] * 2
    scratch += [vmem(ny, 16, LANES, dtype=F32)] * 2
    scratch += [vmem(ny, 8, LANES, dtype=F32)]
    scratch += [vmem(2, nz, deep, width)]
    scratch += [vmem(rows, width)] * 2 + [vmem(1, width, dtype=F32)]
    scratch += [pltpu.SMEM(a.shape, jnp.int32) for a in (tile_rows, tile_cols, tile_count, window)]
    scratch += [pltpu.SemaphoreType.DMA((SEMS,))] * 2 + [pltpu.SemaphoreType.DMA((20,))]
    anywhere = pl.BlockSpec(memory_space=pl.ANY)
    far = pl.BlockSpec(memory_space=pltpu.HBM)
    sizes = (ny, nz, slots, edge, width)
    matrix = jax.ShapeDtypeStruct((rows, width), BF)
    weight = jax.ShapeDtypeStruct((nz, deep, width), BF)
    vector = jax.ShapeDtypeStruct((1, width), F32)
    results = pl.pallas_call(
        functools.partial(layer, sizes),
        out_shape=(matrix, matrix, jax.ShapeDtypeStruct((2, nz, deep, width), BF), vector),
        in_specs=[far] * 10,
        out_specs=(anywhere,) * 4,
        scratch_shapes=scratch,
        compiler_params=pltpu.CompilerParams(
            collective_id=0, has_side_effects=True, vmem_limit_bytes=VMEM_LIMIT
        ),
    )(
        features,
        tile_vals,
        tile_rows,
        tile_cols,
        tile_count,
        window,
        w_neigh,
        w_self,
        layer_bias.reshape(1, width),
        cotangent,
    )
    hidden, gfeat, gneigh, gself, gbias = pl.pallas_call(
        write_out,
        out_shape=(matrix, matrix, weight, weight, vector),
        in_specs=[anywhere] * 4,
        out_specs=(far,) * 5,
        scratch_shapes=[
            vmem(nz, deep, width),
            vmem(nz, deep, width),
            vmem(rows, width),
            vmem(rows, width),
            vmem(1, width, dtype=F32),
            pltpu.SemaphoreType.DMA((10,)),
        ],
        compiler_params=pltpu.CompilerParams(vmem_limit_bytes=VMEM_LIMIT),
    )(*results)
    return hidden, gfeat, gneigh.reshape(width, width), gself.reshape(width, width), gbias.reshape(width)


def solution(mesh):
    in_specs = (
        P(("col", "row"), None),
        P("row", "col", None, None),
        P("row", "col"),
        P("row", "col"),
        P("row", "col"),
        P("row", None),
        P(),
        P(),
        P(),
        P(("col", "row"), None),
    )
    out_specs = (P(("col", "row"), None), P(("col", "row"), None), P(), P(), P())
    return jax.shard_map(
        on_device, mesh=mesh, in_specs=in_specs, out_specs=out_specs, check_vma=False
    )
```

time: 581 us -> 140 us (0.24)
  waiting for transfers between devices: 292 us -> 0 us
  blocking collectives: 183 us -> 0 us
  Pallas kernels: 0 us -> 139 us
  starting transfers between devices: 32.2 us -> 0 us
  matrix products: 26.1 us -> 0 us
  local copies, waits for them, and re-layouts: 19.6 us -> 0 us
  other arithmetic: 13.4 us -> 0 us
  between operations: 14.6 us -> 1.29 us
    psum x1 -> x0, blocking collectives: 183 us -> none  [on_device(): lax.psum((neigh_term, self_term, bias_term), ('row', 'col'))]
    pallas_call x0 -> x2, Pallas kernels: none -> 139 us  [the longest x1 137 us: on_device(): pl.pallas_call(functools.partial(layer, sizes), out_shape=(matrix, matrix...]
    psum x1 -> x0, waiting for transfers between devices: 131 us -> none  [on_device(): lax.psum((neigh_term, self_term, bias_term), ('row', 'col'))]
    all_gather x2 -> x0, waiting for transfers between devices: 113 us -> none  [the longest x1 74.4 us: on_device(): col_panel = lax.all_gather(features, 'row', axis=0, tiled=True)]
    all_to_all x3 -> x0, waiting for transfers between devices: 47.4 us -> none  [the longest x1 47.4 us: on_device(): lax.all_to_all(partial_value.astype(jnp.bfloat16).reshape(col_devs, rows_...]
    all_to_all x3 -> x0, starting transfers between devices: 31.9 us -> none  [the longest x1 11.8 us: on_device(): lax.all_to_all(degree_part.astype(jnp.bfloat16).reshape(col_devs, rows_de...]
    dot_general x12 -> x0, matrix products: 26.1 us -> none  [the longest x1 8.49 us: on_device(): jnp.einsum('mj,mif->jif', col_hot, backward, precision=highest)]
    convert_element_type x6 -> x0, other arithmetic: 8.95 us -> none  [the longest x1 2.77 us: on_device(): grad_self = (sum_self * factor).astype(jnp.bfloat16)]
  transfers between devices with their start and end apart: 6 -> 0, of which waited for: 4 -> 0; matrix products, arithmetic and copies ran while one was open for 5% -> 0% of each run, Pallas kernels for 0% -> 0%
where the time goes in v2:
time: 140 us
  Pallas kernels  139 us (99%)
    pallas_call x1, Pallas kernels, on_device(): pl.pallas_call(functools.partial(layer, sizes), out_shape=(matrix, matrix...  137 us

profile of v2, /device:TPU:1, one launch (start us, length us, event | category | flops | bytes accessed | tf_op | source)
XLA Modules:
  0.0 140.0 jit_solution(8620182445736603255)
XLA Ops:
  1.3 136.6 %shard_map.137 = (bf16[128,512]{1,0:T(8,128)(2,1)}, bf16[128,512]{1,0:T(8,128)(2,1)}, bf16[2,8,64,512]{3,2,1,0:T(8,128)(2,1)}, f32[1,512]{1,0:T(1,128)}) custom-call(bf16[128,512]{1,0:T(8,128)(2,1)} %feat.1, bf16[1,4,256,256]{3,2,1,0:T(8,128)(2,1)} %tiles.1, s32[1,4]{1,0:T(1,128)} %rows_in.1, s32[1,4]{1,0:T(1,128)} %cols_in.1, s32[1,1]{1,0:T(1,128)S(6)} %copy.15.count_in, ...), custom_call_target="tpu_custom_call" | custom-call | tf_op jit(solution)/shard_map/pallas_call | solution.py:918
  137.9 2.2 %shard_map.138 = (bf16[128,512]{1,0:T(8,128)(2,1)}, bf16[128,512]{1,0:T(8,128)(2,1)}, bf16[8,64,512]{2,1,0:T(8,128)(2,1)}, bf16[8,64,512]{2,1,0:T(8,128)(2,1)}, f32[1,512]{1,0:T(1,128)}) custom-call(bf16[128,512]{1,0:T(8,128)(2,1)} %get-tuple-element.14.hidden, bf16[128,512]{1,0:T(8,128)(2,1)} %get-tuple-element.15.gfeat, ...), custom_call_target="tpu_custom_call" | custom-call | tf_op jit(solution)/shard_map/pallas_call | solution.py:939

commit v3 on v2

--- a/solution.py
+++ b/solution.py
@@ -17,12 +17,13 @@
 FWD = ((256, False), (256, False),)
 BWD = ((256, False), (256, False),)
 STAGGER = 0
+TOP_FWD, TOP_BWD = 48, 64
 ROWS = 128
 HALF = ROWS // 2
 LANES = 128
-SEMS = 400
+SEMS = 480
 VMEM_LIMIT = 63 * 1024 * 1024
-LINK_RATE, HOP = 88e3, 1.6
+LINK_RATE, HOP = 88e3, 2.3
 CORE_RATE, CORE_HOP = 350e3, 0.9
 ISSUE = 0.07
 PLANE = 3.5
@@ -157,7 +158,7 @@
             ref = block(owner, None if step < steps else half)
             held = links.start(ref, ref, device(lax.rem(me + way + size, size)), (axis, way))
         if pass_on is not None and (step > 1 or way > 0):
-            pass_on(block(owner, None if step <= steps else half))
+            pass_on(owner, None if step <= steps else half)
     done()
 
 
@@ -344,46 +345,93 @@
             copies.append(links.start(src(other), dst(me), device(other), (axis, way), abs(steps)))
         return copies
 
-    top, low_rows = pl.ds(0, HALF), HALF // 2
+    def lanes_half(ref, at, p, wide):
+        if p is None:
+            return ref.at[at]
+        return ref.at[(*at, pl.ds(p * (wide // 2), wide // 2))]
 
     def gather0(q):
-        def view(o, p):
-            if p is None:
-                return panel[q].at[o, :, top]
-            return panel[q].at[o, pl.ds(XH * p, XH), top]
-
-        mine = panel[q].at[y, x, top]
-        copies = straight("x", NX, x, at_x, lambda o: mine, lambda i: mine)
-        yield max(when for _, when in copies)
-        for copy, _ in copies:
-            copy.wait_recv()
+        rows, wide = pl.ds(0, TOP_FWD), FWD[q][0]
+
+        def along_y(b):
+            for way in (1, -1):
+                chain = gather_chain(
+                    links,
+                    "y",
+                    way,
+                    NY,
+                    y,
+                    lambda o, p: lanes_half(panel[q], (o, b, rows), p, wide),
+                    at_y,
+                    ready_a[q].done,
+                )
+                plan.spawn(chain, plan.now)
+
+        halves = []
+
+        def arrived(b, p):
+            if p is not None:
+                halves.append(b)
+                if len(halves) < 2:
+                    return
+            along_y(b)
+
         for way in (1, -1):
-            plan.spawn(gather_chain(links, "y", way, NY, y, view, at_y, ready_a[q].done), plan.now)
+            chain = gather_chain(
+                links,
+                "x",
+                way,
+                NX,
+                x,
+                lambda o, p: lanes_half(panel[q], (y, o, rows), p, wide),
+                at_x,
+                lambda: None,
+                arrived,
+            )
+            plan.spawn(chain, plan.now)
 
     def gather1(q):
-        deep = NY // 2
-
-        def view(o, p):
-            if p is None:
-                return panel[q].at[:, o, pl.ds(HALF, HALF)]
-            return panel[q].at[pl.ds(deep * p, deep), o, pl.ds(HALF, HALF)]
-
-        def cols_then():
+        rows, wide = pl.ds(TOP_FWD, ROWS - TOP_FWD), FWD[q][0]
+        halves = []
+
+        def along_x(b):
             for way in (1, -1):
-                plan.spawn(gather_chain(links, "x", way, NX, x, view, at_x, ready_a[q].done), plan.now)
-
-        def inner(o, p):
-            if p is None:
-                return panel[q].at[o, x, pl.ds(HALF, HALF)]
-            return panel[q].at[o, x, pl.ds(HALF + low_rows * p, low_rows)]
-
-        mid = Join(2, cols_then)
+                chain = gather_chain(
+                    links,
+                    "x",
+                    way,
+                    NX,
+                    x,
+                    lambda o, p: lanes_half(panel[q], (b, o, rows), p, wide),
+                    at_x,
+                    ready_a[q].done,
+                )
+                plan.spawn(chain, plan.now)
+
+        def arrived(b, p):
+            if p is not None:
+                halves.append(b)
+                if len(halves) < 2:
+                    return
+            along_x(b)
+
         for way in (1, -1):
-            plan.spawn(gather_chain(links, "y", way, NY, y, inner, at_y, mid.done), plan.now)
+            chain = gather_chain(
+                links,
+                "y",
+                way,
+                NY,
+                y,
+                lambda o, p: lanes_half(panel[q], (o, x, rows), p, wide),
+                at_y,
+                lambda: None,
+                arrived,
+            )
+            plan.spawn(chain, plan.now)
 
     def gather(q):
         yield STAGGER * q
-        plan.spawn(gather0(q), plan.now)
+        gather0(q)
         gather1(q)
 
     def take_tiles():
@@ -422,6 +470,8 @@
         own_in[...] = jnp.where((at >= lo) & (at < hi), 1.0, 0.0)
 
     def invert():
+        yield 6.0
+        plan.flush()
         yield 18.0
         degree.wait_recv()
         total = deg_all[0]
@@ -535,11 +585,13 @@
             cols = slice(fwd_at[q], fwd_at[q] + wide)
             lhs[0, :, cols] = low
             pre[...] += nn(low, wnv[cols, :])
+        swaps = [links.start(lhs.at[mate], lhs_in, partner, "core")]
         value = pre[...]
         s = jax.nn.sigmoid(value)
         dpre = cotv[...].astype(F32) * (s * (1.0 + value * (1.0 - s)))
         low = dpre.astype(BF)
         dlow[...] = low
+        swaps.append(links.start(dlow, dlow_in, partner, "core"))
         scale = inv[...] * own_in[...]
         plan.now += 1.5
         for q in bwd:
@@ -554,7 +606,7 @@
         hid[...] = (value * s).astype(BF)
         hidden_store.start()
         plan.now += 0.4
-        plan.spawn(gradients(), plan.now)
+        plan.spawn(gradients(swaps), plan.now)
 
         def self_back():
             selfg[...] = nt(dlow[...], wsv[...])
@@ -567,7 +619,8 @@
         mates = []
         view = cut(back[q], HALF)
 
-        def pass_on(ref):
+        def pass_on(o, p):
+            ref = view(o, k, p)
             mates.append(links.start(ref, ref, partner, "core"))
 
         def then():
@@ -575,7 +628,7 @@
 
         def direct_chain():
             mine = back[q].at[z, k]
-            pass_on(mine)
+            pass_on(z, None)
             copies = []
             for d in sorted(range(1, NZ), key=lambda d: -abs(far(d, NZ)[0])):
                 other = lax.rem(z + d, NZ)
@@ -584,7 +637,7 @@
             for d, copy, when in sorted(copies, key=lambda item: item[2]):
                 yield when
                 copy.wait_recv()
-                pass_on(back[q].at[lax.rem(z - d + NZ, NZ), k])
+                pass_on(lax.rem(z - d + NZ, NZ), None)
             then()
 
         if BWD[q][1]:
@@ -619,6 +672,8 @@
         plan.now += 2.0
         scatter0(q)
         scatter1(q)
+
+    top, low_rows = pl.ds(0, HALF), HALF // 2
 
     def scatter0(q):
         last_y = NY // 2 - 1
@@ -694,24 +749,18 @@
             plan.spawn(chain, plan.now)
 
     def write(q, h, terms):
-        rows, cols = slice(HALF * h, HALF * (h + 1)), slice(bwd_at[q], bwd_at[q] + BWD[q][0])
+        rows = slice(TOP_BWD, ROWS) if h else slice(0, TOP_BWD)
+        cols = slice(bwd_at[q], bwd_at[q] + BWD[q][0])
         total = colp[q][y, x, rows].astype(F32)
         for term in terms:
             total = total + term.astype(F32)
         gft[rows, cols] = (total + selfg[rows, cols]).astype(BF)
 
-    def gradients():
-        swaps = [
-            links.start(lhs.at[mate], lhs_in, partner, "core"),
-            links.start(dlow, dlow_in, partner, "core"),
-            links.start(dbias, dbias_in, partner, "core"),
-        ]
+    def gradients(swaps):
+        meet, when = links.start(dbias, dbias_in, partner, "core")
         yield swaps[-1][1]
         for copy, _ in swaps:
             copy.wait_recv()
-        bz_in[z] = dbias[...] + dbias_in[...]
-        bias_z.start()
-        yield plan.now
         wide = WIDTH // 4
         for i in range(4):
             at = slice(i * wide, (i + 1) * wide)
@@ -739,6 +788,10 @@
                 ),
                 plan.now,
             )
+        yield when
+        meet.wait_recv()
+        bz_in[z] = dbias[...] + dbias_in[...]
+        bias_z.start()
 
     def plane_sum():
         yield plan.now
@@ -783,6 +836,11 @@
         mates = []
         end = Join(2, lambda: plan.spawn(collect(mates), max(when for _, when in mates)))
         view = cut(grads, DEEP // 2)
+
+        def pass_on(o, p):
+            ref = view(k, o, p)
+            mates.append(links.start(ref, ref, partner, "core"))
+
         for way in (1, -1):
             chain = gather_chain(
                 links,
@@ -793,7 +851,7 @@
                 lambda o, p: view(k, o, p),
                 at_z,
                 end.done,
-                lambda ref: mates.append(links.start(ref, ref, partner, "core")),
+                pass_on,
             )
             plan.spawn(chain, plan.now)
 
@@ -820,7 +878,7 @@
         lambda i: grads.at[k, z, :, lanes_of(i)],
     )
 
-    ready_a = [Join(4, lambda q=q: plan.spawn(forward(q), plan.now)) for q in fwd]
+    ready_a = [Join(2 * (NX + NY), lambda q=q: plan.spawn(forward(q), plan.now)) for q in fwd]
     ready_b = Join(len(FWD), lambda: plan.spawn(middle(), plan.now))
     for q in fwd:
         plan.spawn(gather(q), STAGGER * q)
@@ -829,7 +887,7 @@
         plan.later(0.3, functools.partial(turn, m))
     plan.later(1.5, degrees)
     plan.later(1.0, self_term)
-    plan.spawn(invert(), 10.0)
+    plan.spawn(invert(), 2.0)
     plan.run()
     assert links.used <= SEMS
 
@@ -884,10 +942,10 @@
         (bwd, (nz, 2, ROWS)),
         (bwd, (slots + 1, edge)),
         (bwd, (ny, NX, ROWS)),
-        (bwd, (2, ny // 2, NX, HALF)),
-        (bwd, (NX, HALF)),
-        (bwd, (2, NX // 2, ny, HALF)),
-        (bwd, (ny, HALF)),
+        (bwd, (2, ny // 2, NX, TOP_BWD)),
+        (bwd, (NX, TOP_BWD)),
+        (bwd, (2, NX // 2, ny, ROWS - TOP_BWD)),
+        (bwd, (ny, ROWS - TOP_BWD)),
     ]
     deep = width // nz
     scratch = [vmem(*shape, w) for widths, shape in each for w in widths]

time: 140 us -> 134 us (0.957)
  Pallas kernels: 139 us -> 133 us
    pallas_call x1, Pallas kernels: 137 us -> 131 us  [on_device(): pl.pallas_call(functools.partial(layer, sizes), out_shape=(matrix, matrix...]
where the time goes in v3:
time: 134 us
  Pallas kernels  133 us (99%)
    pallas_call x1, Pallas kernels, on_device(): pl.pallas_call(functools.partial(layer, sizes), out_shape=(matrix, matrix...  131 us

profile of v3, /device:TPU:1, one launch (start us, length us, event | category | flops | bytes accessed | tf_op | source)
XLA Modules:
  0.0 134.3 jit_solution(11301835199953417094)
XLA Ops:
  1.3 130.9 %shard_map.137 = (bf16[128,512]{1,0:T(8,128)(2,1)}, bf16[128,512]{1,0:T(8,128)(2,1)}, bf16[2,8,64,512]{3,2,1,0:T(8,128)(2,1)}, f32[1,512]{1,0:T(1,128)}) custom-call(bf16[128,512]{1,0:T(8,128)(2,1)} %feat.1, bf16[1,4,256,256]{3,2,1,0:T(8,128)(2,1)} %tiles.1, s32[1,4]{1,0:T(1,128)} %rows_in.1, s32[1,4]{1,0:T(1,128)} %cols_in.1, s32[1,1]{1,0:T(1,128)S(6)} %copy.15.count_in, ...), custom_call_target="tpu_custom_call" | custom-call | tf_op jit(solution)/shard_map/pallas_call | solution.py:976
  132.1 2.2 %shard_map.138 = (bf16[128,512]{1,0:T(8,128)(2,1)}, bf16[128,512]{1,0:T(8,128)(2,1)}, bf16[8,64,512]{2,1,0:T(8,128)(2,1)}, bf16[8,64,512]{2,1,0:T(8,128)(2,1)}, f32[1,512]{1,0:T(1,128)}) custom-call(bf16[128,512]{1,0:T(8,128)(2,1)} %get-tuple-element.14.hidden, bf16[128,512]{1,0:T(8,128)(2,1)} %get-tuple-element.15.gfeat, ...), custom_call_target="tpu_custom_call" | custom-call | tf_op jit(solution)/shard_map/pallas_call | solution.py:997

commit v4 on v3

--- a/solution.py
+++ b/solution.py
@@ -23,10 +23,10 @@
 LANES = 128
 SEMS = 480
 VMEM_LIMIT = 63 * 1024 * 1024
-LINK_RATE, HOP = 88e3, 2.3
+LINK_RATE, HOP = 80e3, 2.8
 CORE_RATE, CORE_HOP = 350e3, 0.9
 ISSUE = 0.07
-PLANE = 3.5
+PLANE = 4.5
 
 
 def nn(a, b):

time: 134 us -> 131 us (0.978)
  Pallas kernels: 133 us -> 130 us
    pallas_call x1, Pallas kernels: 131 us -> 127 us  [on_device(): pl.pallas_call(functools.partial(layer, sizes), out_shape=(matrix, matrix...]
where the time goes in v4:
time: 131 us
  Pallas kernels  130 us (99%)
    pallas_call x1, Pallas kernels, on_device(): pl.pallas_call(functools.partial(layer, sizes), out_shape=(matrix, matrix...  127 us

profile of v4, /device:TPU:1, one launch (start us, length us, event | category | flops | bytes accessed | tf_op | source)
XLA Modules:
  0.0 130.9 jit_solution(3475063144855063288)
XLA Ops:
  1.3 127.4 %shard_map.137 = (bf16[128,512]{1,0:T(8,128)(2,1)}, bf16[128,512]{1,0:T(8,128)(2,1)}, bf16[2,8,64,512]{3,2,1,0:T(8,128)(2,1)}, f32[1,512]{1,0:T(1,128)}) custom-call(bf16[128,512]{1,0:T(8,128)(2,1)} %feat.1, bf16[1,4,256,256]{3,2,1,0:T(8,128)(2,1)} %tiles.1, s32[1,4]{1,0:T(1,128)} %rows_in.1, s32[1,4]{1,0:T(1,128)} %cols_in.1, s32[1,1]{1,0:T(1,128)S(6)} %copy.15.count_in, ...), custom_call_target="tpu_custom_call" | custom-call | tf_op jit(solution)/shard_map/pallas_call | solution.py:976
  128.7 2.2 %shard_map.138 = (bf16[128,512]{1,0:T(8,128)(2,1)}, bf16[128,512]{1,0:T(8,128)(2,1)}, bf16[8,64,512]{2,1,0:T(8,128)(2,1)}, bf16[8,64,512]{2,1,0:T(8,128)(2,1)}, f32[1,512]{1,0:T(1,128)}) custom-call(bf16[128,512]{1,0:T(8,128)(2,1)} %get-tuple-element.14.hidden, bf16[128,512]{1,0:T(8,128)(2,1)} %get-tuple-element.15.gfeat, ...), custom_call_target="tpu_custom_call" | custom-call | tf_op jit(solution)/shard_map/pallas_call | solution.py:997

commit v5 on v4

--- a/solution.py
+++ b/solution.py
@@ -23,10 +23,10 @@
 LANES = 128
 SEMS = 480
 VMEM_LIMIT = 63 * 1024 * 1024
-LINK_RATE, HOP = 80e3, 2.8
+LINK_RATE, HOP = 80e3, 3.0
 CORE_RATE, CORE_HOP = 350e3, 0.9
 ISSUE = 0.07
-PLANE = 4.5
+PLANE = 5.0
 
 
 def nn(a, b):

time: 131 us -> 131 us (level)
  no operation moved by 1% of the time
where the time goes in v5:
time: 131 us; the launch traced here: 130 us
  Pallas kernels  129 us (98%)
    pallas_call x1, Pallas kernels, on_device(): pl.pallas_call(functools.partial(layer, sizes), out_shape=(matrix, matrix...  127 us

profile of v5, /device:TPU:1, one launch (start us, length us, event | category | flops | bytes accessed | tf_op | source)
XLA Modules:
  0.0 130.3 jit_solution(6807508863797298025)
XLA Ops:
  1.3 126.8 %shard_map.137 = (bf16[128,512]{1,0:T(8,128)(2,1)}, bf16[128,512]{1,0:T(8,128)(2,1)}, bf16[2,8,64,512]{3,2,1,0:T(8,128)(2,1)}, f32[1,512]{1,0:T(1,128)}) custom-call(bf16[128,512]{1,0:T(8,128)(2,1)} %feat.1, bf16[1,4,256,256]{3,2,1,0:T(8,128)(2,1)} %tiles.1, s32[1,4]{1,0:T(1,128)} %rows_in.1, s32[1,4]{1,0:T(1,128)} %cols_in.1, s32[1,1]{1,0:T(1,128)S(6)} %copy.15.count_in, ...), custom_call_target="tpu_custom_call" | custom-call | tf_op jit(solution)/shard_map/pallas_call | solution.py:976
  128.1 2.2 %shard_map.138 = (bf16[128,512]{1,0:T(8,128)(2,1)}, bf16[128,512]{1,0:T(8,128)(2,1)}, bf16[8,64,512]{2,1,0:T(8,128)(2,1)}, bf16[8,64,512]{2,1,0:T(8,128)(2,1)}, f32[1,512]{1,0:T(1,128)}) custom-call(bf16[128,512]{1,0:T(8,128)(2,1)} %get-tuple-element.14.hidden, bf16[128,512]{1,0:T(8,128)(2,1)} %get-tuple-element.15.gfeat, ...), custom_call_target="tpu_custom_call" | custom-call | tf_op jit(solution)/shard_map/pallas_call | solution.py:997
